TPU v7x, 512 devices: a whole 4x4x16 slice. The times are simulated.
512 devices in a mesh: tile: 64 (over z, y), mem: 8 (over x, core).
Axes of the slice: x: 4, y: 4, z: 16, core: 2. Of those that a mesh axis runs over, the one named last changes fastest.
Arguments:
- search_dir: float32 [5, 64, 128, 256], P(None, 'mem', 'tile'), may hold values from -6 to 6
- perturb: bfloat16 [5, 64, 128, 128, 256], P(None, None, 'mem', 'tile'), may hold values from -6 to 6
- smooth_y: float32 [128, 128], replicated, may hold values from -1 to 1
- smooth_x: float32 [256, 256], replicated, may hold values from -1 to 1
- vertical: float32 [64, 64], replicated, may hold values from -1 to 1
- level_scale: int32 [64], replicated, may hold values from 1 to 4
Outputs:
- increment: float32 [5, 64, 128, 256], P(None, 'mem', 'tile')
All inputs are finite; a program needn't handle non-finite values.
Results may differ from a plain program's by a relative error of at most 0.0003.
Values sent between devices are 32-bit elements; how exact they have to be, the bound alone decides.
No kernel may reach another device: no remote copies, remote signals or barrier semaphores. Data moves between devices by JAX's collectives and lax.ppermute only.
A program may use at most 128 MiB of HBM per device.

v0:
```python
import jax
import jax.numpy as jnp
from jax import lax
from jax.sharding import PartitionSpec as P

PMAX = 4


def power_stack(matrix):
    highest = lax.Precision.HIGHEST
    power = jnp.eye(matrix.shape[0], dtype=jnp.float32)
    result = []
    for step in range(PMAX):
        power = jnp.dot(matrix, power, precision=highest)
        result.append(jnp.dot(power, power.T, precision=highest))
    return jnp.stack(result)


def per_device(search_dir, perturb, smooth_y, smooth_x, vertical, level_scale):
    highest = lax.Precision.HIGHEST
    full_dir = lax.all_gather(search_dir, "mem", axis=1, tiled=True)
    members = perturb.shape[2]
    levels = full_dir.shape[1]
    rows = full_dir.shape[2]
    width = full_dir.shape[3]
    controls = jnp.sum(perturb.astype(jnp.float32) * full_dir[:, :, None], axis=0)
    adjoint = lax.dot_general(
        vertical, controls.reshape(levels, -1), (((0,), (0,)), ((), ())), precision=highest
    )
    adjoint = adjoint.reshape(levels, members, rows, width)
    tiles = lax.axis_size("tile")
    fields = adjoint.reshape(levels * members, rows, width)
    counts = jnp.repeat(level_scale, members, total_repeat_length=levels * members)
    per_owner = fields.shape[0] // tiles
    owned = lax.all_to_all(fields, "tile", split_axis=0, concat_axis=1, tiled=True)
    own_counts = lax.dynamic_slice_in_dim(counts, lax.axis_index("tile") * per_owner, per_owner)
    pick_y = jnp.take(power_stack(smooth_y), own_counts - 1, axis=0)
    pick_x = jnp.take(power_stack(smooth_x), own_counts - 1, axis=0)
    smoothed = jnp.einsum("fij,fjx->fix", pick_y, owned, precision=highest)
    smoothed = jnp.einsum("fyj,fjx->fyx", smoothed, pick_x, precision=highest)
    returned = lax.all_to_all(smoothed, "tile", split_axis=1, concat_axis=0, tiled=True)
    returned = returned.reshape(levels, members, rows, width)
    forward = jnp.dot(vertical, returned.reshape(levels, -1), precision=highest)
    forward = forward.reshape(levels, members, rows, width)
    terms = jnp.sum(perturb.astype(jnp.float32) * forward[None], axis=2)
    total_members = members * lax.axis_size("mem")
    share = lax.psum_scatter(terms, "mem", scatter_dimension=1, tiled=True)
    return share / (total_members - 1)


def solution(mesh):
    in_specs = (
        P(None, "mem", "tile", None),
        P(None, None, "mem", "tile", None),
        P(),
        P(),
        P(),
        P(),
    )
    out_specs = P(None, "mem", "tile", None)
    return jax.shard_map(
        per_device, mesh=mesh, in_specs=in_specs, out_specs=out_specs, check_vma=False
    )
```

profile of v0, /device:TPU:1, one launch (start us, length us, event | category | flops | bytes accessed | tf_op | source)
XLA Modules:
  0.0 337.0 jit_solution(14902512583073721843)
XLA Ops:
  6.5 20.3 %all_gather.3 = f32[5,64,2,256]{3,2,1,0:T(2,128)S(1)} all-gather(f32[5,8,2,256]{3,2,1,0:T(2,128)} %param.8), channel_id=1, replica_groups=mesh['tile'=64,'mem'=8] {'mem'}, dimensions={1}, use_global_device_ids=true | all-gather | bytes 737280 | tf_op jit(solution)/shard_map/all_gather | solution.py:21
  26.8 13.1 %fusion = f32[64,16,2,256]{3,2,1,0:T(2,128)} fusion(bf16[5,64,16,2,256]{4,3,2,1,0:T(2,128)(2,1)} %param.9, f32[5,64,2,256]{3,2,1,0:T(2,128)S(1)} %all_gather.3), kind=kLoop, calls=%fused_computation.4 | loop fusion | flops 7340032 | bytes 7995392 | tf_op jit(solution)/shard_map/reduce_sum | solution.py:26
  39.9 2.9 reshape.91
  42.8 3.4 convolution_bitcast_fusion.1
  46.2 4.0 %reshape_reshape.6 = f32[1024,2,256]{2,1,0:T(2,128)} reshape(f32[64,8192]{1,0:T(8,128)} %convolution_bitcast_fusion.1) | data formatting | bytes 4194304 | tf_op jit(solution)/shard_map/reshape;reshape | solution.py:32
  50.2 13.6 %all-to-all-start = ((f32[1024,2,256]{2,1,0:T(2,128)}), f32[1024,2,256]{2,1,0:T(2,128)S(1)}, u32[]{:S(2)}, u32[]{:S(2)}) async-start(f32[1024,2,256]{2,1,0:T(2,128)} %reshape_reshape.6), calls=%async_computation | async-start | bytes 4194304 | tf_op jit(solution)/shard_map/all_to_all | solution.py:35
  67.0 4.3 %compare_select_fusion.1 = (s32[1024,1]{0,1:T(1,128)S(1)}, s32[1024,1]{0,1:T(1,128)S(1)}) fusion(s32[]{:T(128)} %bitcast.61, s32[]{:T(128)} %bitcast.62, s32[]{:T(128)} %bitcast.63, s32[]{:T(128)} %bitcast.64, s32[]{:T(128)} %bitcast.65, s32[]{:T(128)} %bitcast.67, s32[]{:T(128)} %bitcast.66, s32[1024,1]{0,1:T(1,128)S(1)} %bitcast.151, ...), kind=kLoop, calls=%fused_computation.94 | loop fusion | flops 14336 | bytes 16412 | tf_op jit(solution)/shard_map/jit(_take)/gather | solution.py:33
  72.0 35.6 %select_select_fusion = s32[1024]{0:T(1024)S(1)} fusion(pred[1024]{0:T(1024)(128)(4,1)S(1)} %get-tuple-element.73, pred[1024]{0:T(1024)(128)(4,1)S(1)} %get-tuple-element.72, pred[1024]{0:T(1024)(128)(4,1)S(1)} %get-tuple-element.71, pred[1024]{0:T(1024)(128)(4,1)S(1)} %get-tuple-element.70, pred[1024]{0:T(1024)(128)(4,1)S(1)} %get-tuple-element.69, ...), kind=kLoop, calls=%fused_computation.104 | loop fusion | flops 67584 | bytes 70916 | tf_op jit(solution)/shard_map/jit(_take)/select_n | solution.py:33
  110.0 1.6 gather_fusion
  115.7 2.7 gather_fusion.1
  118.4 42.4 %all-to-all-done = f32[1024,2,256]{2,1,0:T(2,128)S(1)} async-done(((f32[1024,2,256]{2,1,0:T(2,128)}), f32[1024,2,256]{2,1,0:T(2,128)S(1)}, u32[]{:S(2)}, u32[]{:S(2)}) %all-to-all-start) | async-done | bytes 2097184 | tf_op jit(solution)/shard_map/all_to_all | solution.py:35
  161.2 1.0 copy-done.2
  162.2 3.0 fusion.4
  165.3 3.0 fusion.2
  168.3 1.2 copy.15
  169.6 103.1 %all_to_all.33 = f32[16,128,256]{2,0,1:T(8,128)S(1)} all-to-all(f32[16,128,256]{2,0,1:T(8,128)S(1)} %copy.15), channel_id=1, replica_groups=mesh['tile'=64,'mem'=8] {'tile'}, dimensions={1} | all-to-all | bytes 4194304 | tf_op jit(solution)/shard_map/all_to_all | solution.py:41
  272.6 1.9 copy.24
  274.6 2.7 reshape_reshape.7
  277.3 3.6 %convolution_bitcast_fusion = f32[64,8192]{1,0:T(8,128)S(1)} fusion(f32[64,8192]{1,0:T(8,128)} %reshape_reshape.7, f32[64,64]{1,0:T(8,128)S(1)} %copy-done.5), kind=kOutput, calls=%fused_computation.6 | convolution fusion | flops 402653184 | bytes 4210688 | tf_op jit(solution)/shard_map/dot_general | solution.py:43
  280.9 2.8 mul.24
  283.7 9.1 %fusion.1 = f32[5,64,2,256]{3,2,1,0:T(2,128)S(1)} fusion(bf16[5,64,16,2,256]{4,3,2,1,0:T(2,128)(2,1)} %param.9, f32[64,16,2,256]{3,2,1,0:T(2,128)} %mul.24), kind=kLoop, calls=%fused_computation.5 | loop fusion | flops 7700480 | bytes 7995392 | tf_op jit(solution)/shard_map/reduce_sum | solution.py:45
  293.1 1.4 reshape.322
  294.4 34.1 %reduce-scatter.4.cloned.1.call-done = f32[8,2560]{1,0:T(8,128)} async-done(((f32[64,2560]{1,0:T(8,128)}), f32[8,2560]{1,0:T(8,128)}) %reduce-scatter.4.cloned.1.call-update) | async-done | bytes 81936
  328.5 0.9 reshape.323
  (46 shorter events, 11.4 us)
Async XLA Ops:
  6.5 105.1 %copy-start = (f32[256,256]{1,0:T(8,128)S(1)}, f32[256,256]{1,0:T(8,128)}, u32[]{:S(2)}) copy-start(f32[256,256]{1,0:T(8,128)} %param.11) | copy-start | bytes 786436
  39.9 2.9 copy-start.5
  50.2 13.8 %copy-start.3 = (s32[64]{0:T(128)S(1)}, s32[64]{0:T(128)}, u32[]{:S(2)}) copy-start(s32[64]{0:T(128)} %param.13) | copy-start | bytes 772
  50.2 16.7 %copy-start.6 = (s32[8,128]{1,0:T(8,128)S(1)}, s32[8,128]{1,0:T(8,128)}, u32[]{:S(2)}) copy-start(s32[8,128]{1,0:T(8,128)} %constant.118.clone.1) | copy-start | bytes 12292
  50.2 57.5 %copy-start.4 = (f32[128,128]{1,0:T(8,128)S(1)}, f32[128,128]{1,0:T(8,128)}, u32[]{:S(2)}) copy-start(f32[128,128]{1,0:T(8,128)} %param.10) | copy-start | bytes 196612
  50.2 110.6 %all-to-all-start = ((f32[1024,2,256]{2,1,0:T(2,128)}), f32[1024,2,256]{2,1,0:T(2,128)S(1)}, u32[]{:S(2)}, u32[]{:S(2)}) async-start(f32[1024,2,256]{2,1,0:T(2,128)} %reshape_reshape.6), calls=%async_computation | async-start | bytes 4194304 | tf_op jit(solution)/shard_map/all_to_all | solution.py:35
  63.8 264.7 %reduce-scatter.4.cloned.1.call-start = ((), (), s32[]{:S(2)}) async-start(), calls=%async_computation.3 | async-start | bytes 737280
  161.0 1.2 copy-start.2
  162.2 3.1 copy-start.1
Sparse Core Ops, SparseCore 0:
  294.6 33.9 reduce-scatter.3
where the time goes:
time: 339 us; the launch traced here: 337 us
  blocking collectives  123 us (36%)
  waiting for transfers between devices  76.5 us (23%)
  other arithmetic  63.7 us (19%)
  local copies, waits for them, and re-layouts  26.8 us (8%)
  matrix products  19.1 us (6%)
  starting transfers between devices  13.8 us (4%)
  between operations  13.7 us (4%)
    all_to_all x1, blocking collectives, per_device(): lax.all_to_all(smoothed, 'tile', split_axis=1, concat_axis=0, tiled=True)  103 us
    all_to_all x1, waiting for transfers between devices, per_device(): lax.all_to_all(fields, 'tile', split_axis=0, concat_axis=1, tiled=True)  42.4 us
    select_n x1, other arithmetic, per_device(): jnp.repeat(level_scale, members, total_repeat_length=levels * members)  35.6 us
    unnamed x2, waiting for transfers between devices  34.1 us
    all_gather x1, blocking collectives, per_device(): full_dir = lax.all_gather(search_dir, 'mem', axis=1, tiled=True)  20.3 us
    all_to_all x1, starting transfers between devices, per_device(): lax.all_to_all(fields, 'tile', split_axis=0, concat_axis=1, tiled=True)  13.6 us
    reduce_sum x1, other arithmetic, per_device(): jnp.sum(perturb.astype(jnp.float32) * full_dir[:, :, None], axis=0)  13.1 us
    reduce_sum x1, other arithmetic, per_device(): terms = jnp.sum(perturb.astype(jnp.float32) * forward[None], axis=2)  9.07 us
  transfers between devices with their start and end apart: 2, of which 2 were waited for; matrix products, arithmetic and copies ran while one was open for 16% of the time, Pallas kernels for 0%

commit v1 on v0

v1 whole, which is shorter than its diff:
```python
import jax
import jax.numpy as jnp
from jax import lax
from jax.experimental import pallas as pl
from jax.experimental.pallas import tpu as pltpu
from jax.sharding import PartitionSpec as P

F32 = jnp.float32
BF16 = jnp.bfloat16
VMEM_LIMIT = 50 * 1024 * 1024
LEVELS = 64
VARS = 5
ROWS = 64
CHUNK = 16
STEPS = ROWS // CHUNK


def split(value):
    high = value.astype(BF16)
    low = (value - high.astype(F32)).astype(BF16)
    return high, low


def dot(a, b):
    return jnp.dot(a, b, preferred_element_type=F32)


def vertical_product(matrix, source, target):
    m_high, m_low = split(matrix)
    left = jnp.concatenate([m_high, m_high, m_low], axis=1)
    for pair in range(CHUNK // 2):
        parts = [source[pl.ds(2 * pair + i, LEVELS, stride=CHUNK), :] for i in range(2)]
        high, low = split(jnp.concatenate(parts, axis=1))
        result = dot(left, jnp.concatenate([high, low, high], axis=0))
        for i in range(2):
            target[pl.ds(2 * pair + i, LEVELS, stride=CHUNK), :] = result[:, 128 * i : 128 * (i + 1)]


def adjoint_kernel(dir_ref, perturb_ref, matrix_ref, out_ref, controls, result):
    def level(q, carry):
        total = None
        for v in range(VARS):
            direction = dir_ref[v, q]
            direction = jnp.concatenate([direction] * (CHUNK // 4), axis=0)
            term = perturb_ref[v, q].astype(F32) * direction
            total = term if total is None else total + term
        controls[pl.ds(pl.multiple_of(q * CHUNK, CHUNK), CHUNK), :] = total
        return carry

    lax.fori_loop(0, LEVELS, level, 0, unroll=4)
    vertical_product(matrix_ref[...], controls, result)
    out_ref[...] = result[...].reshape(LEVELS, CHUNK, 128)


def prepare_kernel(scale_ref, smooth_y_ref, smooth_x_ref, y_ref, xh_ref, xl_ref):
    scale = scale_ref[0]

    def covariance(matrix):
        power = matrix
        chosen = matrix
        for step in range(2, 5):
            power = jnp.dot(matrix, power, precision=lax.Precision.HIGHEST, preferred_element_type=F32)
            chosen = jnp.where(scale == step, power, chosen)
        return lax.dot_general(
            chosen, chosen, (((1,), (1,)), ((), ())), precision=lax.Precision.HIGHEST, preferred_element_type=F32
        )

    high, low = split(covariance(smooth_y_ref[...]))
    y_ref[...] = jnp.concatenate([high, high, low], axis=1)
    high, low = split(covariance(smooth_x_ref[...]))
    xh_ref[...] = high
    xl_ref[...] = low


def smooth_kernel(in_ref, y_ref, xh_ref, xl_ref, out_ref, source, target):
    source[...] = in_ref[...].reshape(LEVELS * CHUNK, 128)
    xh, xl = xh_ref[...], xl_ref[...]
    y_both, y_low = y_ref[:, :256], y_ref[:, 256:]
    for k in range(CHUNK // 4):
        halves = []
        for r in range(2):
            parts = [source[pl.ds(4 * k + 2 * half + r, LEVELS, stride=CHUNK), :] for half in range(2)]
            halves.append(jnp.concatenate(parts, axis=1))
        high, low = split(jnp.concatenate(halves, axis=0))
        along_x = dot(high, xh) + dot(low, xh) + dot(high, xl)
        high, low = split(along_x)
        result = dot(y_both, jnp.concatenate([high, low], axis=0)) + dot(y_low, high)
        for r in range(2):
            for half in range(2):
                target[pl.ds(4 * k + 2 * half + r, LEVELS, stride=CHUNK), :] = result[
                    64 * r : 64 * (r + 1), 128 * half : 128 * (half + 1)
                ]
    out_ref[...] = target[...].reshape(LEVELS, CHUNK, 128)


def increment_kernel(place_ref, in_ref, perturb_ref, matrix_ref, give_ref, keep_ref, source, forward, total):
    step = pl.program_id(0)
    source[...] = in_ref[...].reshape(LEVELS * CHUNK, 128)
    vertical_product(matrix_ref[...], source, forward)

    @pl.when(step == 0)
    def _():
        total[...] = jnp.zeros_like(total)

    def level(q, carry):
        field = forward[pl.ds(pl.multiple_of(q * CHUNK, CHUNK), CHUNK), :]
        for v in range(VARS):
            term = perturb_ref[v, q].astype(F32) * field
            total[v, q] += term[:8] + term[8:]
        return carry

    lax.fori_loop(0, LEVELS, level, 0, unroll=4)

    @pl.when(step == STEPS - 1)
    def _():
        chip, core = place_ref[0], place_ref[1]
        for j in range(4):
            block = lax.rem(chip + j, 4) * 16
            for ref, parity in ((keep_ref, core), (give_ref, 1 - core)):

                def fold(i, carry, ref=ref, base=block + 8 * parity, j=j):
                    for v in range(VARS):
                        both = total[v, base + i]
                        ref[j, v, i] = both[:4] + both[4:]
                    return carry

                lax.fori_loop(0, 8, fold, 0)


def whole(shape):
    return pl.BlockSpec(shape, lambda i: (0,) * len(shape))


PERTURB_BLOCK = pl.BlockSpec((VARS, LEVELS, CHUNK, 128), lambda i: (0, 0, i, 0))
FIELD_BLOCK = pl.BlockSpec((LEVELS, CHUNK, 128), lambda i: (0, i, 0))
FIELDS = jax.ShapeDtypeStruct((LEVELS, ROWS, 128), F32)
FIELD_SCRATCH = pltpu.VMEM((LEVELS * CHUNK, 128), F32)
PARAMS = pltpu.CompilerParams(vmem_limit_bytes=VMEM_LIMIT)


def to_lines(array):
    lead = array.shape[:-2]
    n = len(lead)
    array = array.reshape(lead + (2, 2, 128))
    return array.transpose(tuple(range(n)) + (n + 1, n, n + 2)).reshape(lead + (4, 128))


def per_device(search_dir, perturb, smooth_y, smooth_x, vertical, level_scale):
    mem = lax.axis_index("mem")
    chip, core = mem // 2, mem % 2
    lines = to_lines(perturb).reshape(VARS, LEVELS, ROWS, 128)
    full_dir = lax.all_gather(to_lines(search_dir), "mem", axis=1, tiled=True)
    adjoint = pl.pallas_call(
        adjoint_kernel,
        grid=(STEPS,),
        in_specs=[whole((VARS, LEVELS, 4, 128)), PERTURB_BLOCK, whole((64, 64))],
        out_specs=FIELD_BLOCK,
        out_shape=FIELDS,
        scratch_shapes=[FIELD_SCRATCH, FIELD_SCRATCH],
        compiler_params=PARAMS,
        cost_estimate=pl.CostEstimate(flops=200_000_000, bytes_accessed=8_000_000, transcendentals=0),
        name="adjoint",
    )(full_dir, lines, vertical.T)

    scale = lax.dynamic_slice_in_dim(level_scale, lax.axis_index("tile"), 1)
    ordered_y = smooth_y.reshape(64, 2, 64, 2).transpose(1, 0, 3, 2).reshape(128, 128)
    vmem = pl.BlockSpec(memory_space=pltpu.VMEM)
    cov_y, cov_xh, cov_xl = pl.pallas_call(
        prepare_kernel,
        in_specs=[pl.BlockSpec(memory_space=pltpu.SMEM), vmem, vmem],
        out_specs=[vmem, vmem, vmem],
        out_shape=[
            jax.ShapeDtypeStruct((128, 384), BF16),
            jax.ShapeDtypeStruct((256, 256), BF16),
            jax.ShapeDtypeStruct((256, 256), BF16),
        ],
        compiler_params=PARAMS,
        cost_estimate=pl.CostEstimate(flops=1_000_000_000, bytes_accessed=1_000_000, transcendentals=0),
        name="prepare",
    )(scale, ordered_y, smooth_x)

    owned = lax.all_to_all(adjoint, "tile", split_axis=0, concat_axis=0, tiled=True)
    smoothed = pl.pallas_call(
        smooth_kernel,
        grid=(STEPS,),
        in_specs=[FIELD_BLOCK, whole((128, 384)), whole((256, 256)), whole((256, 256))],
        out_specs=FIELD_BLOCK,
        out_shape=FIELDS,
        scratch_shapes=[FIELD_SCRATCH, FIELD_SCRATCH],
        compiler_params=PARAMS,
        cost_estimate=pl.CostEstimate(flops=1_200_000_000, bytes_accessed=4_000_000, transcendentals=0),
        name="smooth",
    )(owned, cov_y, cov_xh, cov_xl)
    returned = lax.all_to_all(smoothed, "tile", split_axis=0, concat_axis=0, tiled=True)

    share = jax.ShapeDtypeStruct((4, VARS, 8, 4, 128), F32)
    give, keep = pl.pallas_call(
        increment_kernel,
        grid=(STEPS,),
        in_specs=[pl.BlockSpec(memory_space=pltpu.SMEM), FIELD_BLOCK, PERTURB_BLOCK, whole((64, 64))],
        out_specs=[whole(share.shape), whole(share.shape)],
        out_shape=[share, share],
        scratch_shapes=[FIELD_SCRATCH, FIELD_SCRATCH, pltpu.VMEM((VARS, LEVELS, 8, 128), F32)],
        compiler_params=PARAMS,
        cost_estimate=pl.CostEstimate(flops=200_000_000, bytes_accessed=8_000_000, transcendentals=0),
        name="increment",
    )(jnp.stack([chip, core]), returned, lines, vertical)

    other = lax.ppermute(give, "mem", [(m, m ^ 1) for m in range(8)])
    pieces = [keep[j] + other[j] for j in range(4)]
    total = pieces[0]
    for j in (2, 1, 3):
        total = total + lax.ppermute(pieces[j], "mem", [(m, (m + 2 * j) % 8) for m in range(8)])
    total = total / (128 - 1)
    total = total.reshape(VARS, 8, 2, 2, 128).transpose(0, 1, 3, 2, 4)
    return total.reshape(VARS, 8, 2, 256)


def solution(mesh):
    in_specs = (
        P(None, "mem", "tile", None),
        P(None, None, "mem", "tile", None),
        P(),
        P(),
        P(),
        P(),
    )
    out_specs = P(None, "mem", "tile", None)
    return jax.shard_map(
        per_device, mesh=mesh, in_specs=in_specs, out_specs=out_specs, check_vma=False
    )
```

time: 339 us -> 279 us (0.82)
  waiting for transfers between devices: 76.5 us -> 182 us
  blocking collectives: 123 us -> 20.2 us
  other arithmetic: 63.7 us -> 0.84 us
  starting transfers between devices: 13.8 us -> 40.2 us
  Pallas kernels: 0 us -> 22.4 us
  matrix products: 19.1 us -> 0 us
  local copies, waits for them, and re-layouts: 26.8 us -> 11.4 us
  between operations: 13.7 us -> 0.13 us
    all_to_all x1 -> x2, waiting for transfers between devices: 42.4 us -> 179 us  [the longest x1 94.7 us: per_device(): lax.all_to_all(smoothed, 'tile', split_axis=0, concat_axis=0, tiled=True)]
    all_to_all x1 -> x0, blocking collectives: 103 us -> none  [per_device(): lax.all_to_all(smoothed, 'tile', split_axis=1, concat_axis=0, tiled=True)]
    select_n x1 -> x0, other arithmetic: 35.6 us -> none  [per_device(): jnp.repeat(level_scale, members, total_repeat_length=levels * members)]
    unnamed x2 -> x0, waiting for transfers between devices: 34.1 us -> none
    pallas_call x0 -> x4, Pallas kernels: none -> 22.4 us  [the longest x1 6.82 us: per_device(): pl.pallas_call(smooth_kernel, grid=(STEPS,), in_specs=[FIELD_BLOCK, whole...]
    reduce_sum x2 -> x0, other arithmetic: 22.1 us -> none  [the longest x1 13.1 us: per_device(): jnp.sum(perturb.astype(jnp.float32) * full_dir[:, :, None], axis=0)]
    dot_general x20 -> x0, matrix products: 19.1 us -> none  [the longest x1 3.59 us: per_device(): forward = jnp.dot(vertical, returned.reshape(levels, -1), precision=highest)]
    ppermute x0 -> x4, starting transfers between devices: none -> 17.9 us  [the longest x3 9.58 us: per_device(): lax.ppermute(pieces[j], 'mem', [(m, (m + 2 * j) % 8) for m in range(8)])]
  transfers between devices with their start and end apart: 2 -> 6, of which waited for: 2 -> 4; matrix products, arithmetic and copies ran while one was open for 16% -> 3% of each run, Pallas kernels for 0% -> 1%
where the time goes in v1:
time: 279 us; the launch traced here: 277 us
  waiting for transfers between devices  182 us (65%)
  starting transfers between devices  40.2 us (14%)
  Pallas kernels  22.4 us (8%)
  blocking collectives  20.2 us (7%)
  local copies, waits for them, and re-layouts  11.4 us (4%)
    all_to_all x1, waiting for transfers between devices, per_device(): lax.all_to_all(smoothed, 'tile', split_axis=0, concat_axis=0, tiled=True)  94.7 us
    all_to_all x1, waiting for transfers between devices, per_device(): lax.all_to_all(adjoint, 'tile', split_axis=0, concat_axis=0, tiled=True)  84.4 us
    all_gather x1, blocking collectives, per_device(): full_dir = lax.all_gather(to_lines(search_dir), 'mem', axis=1, tiled=True)  20.2 us
    all_to_all x1, starting transfers between devices, per_device(): lax.all_to_all(adjoint, 'tile', split_axis=0, concat_axis=0, tiled=True)  13.6 us
    ppermute x3, starting transfers between devices, per_device(): lax.ppermute(pieces[j], 'mem', [(m, (m + 2 * j) % 8) for m in range(8)])  9.58 us
    all_to_all x1, starting transfers between devices, per_device(): lax.all_to_all(smoothed, 'tile', split_axis=0, concat_axis=0, tiled=True)  8.67 us
    ppermute x1, starting transfers between devices, per_device(): other = lax.ppermute(give, 'mem', [(m, m ^ 1) for m in range(8)])  8.35 us
    pallas_call x1, Pallas kernels, per_device(): pl.pallas_call(smooth_kernel, grid=(STEPS,), in_specs=[FIELD_BLOCK, whole...  6.82 us
  transfers between devices with their start and end apart: 6, of which 4 were waited for; matrix products, arithmetic and copies ran while one was open for 3% of the time, Pallas kernels for 1%

profile of v1, /device:TPU:1, one launch (start us, length us, event | category | flops | bytes accessed | tf_op | source)
XLA Modules:
  0.0 277.5 jit_solution(11923493965721066452)
XLA Ops:
  0.0 20.2 %all_gather.3.dir_ref = f32[5,64,4,128]{3,2,1,0:T(4,128)S(1)} all-gather(f32[5,8,4,128]{3,2,1,0:T(4,128)} %bitcast.39), channel_id=1, replica_groups=mesh['tile'=64,'mem'=8] {'mem'}, dimensions={1}, use_global_device_ids=true | all-gather | bytes 737280 | tf_op jit(solution)/shard_map/all_gather | solution.py:152
  20.2 0.8 copy.14
  21.0 6.4 %adjoint.1 = f32[64,64,128]{2,1,0:T(8,128)} custom-call(f32[5,64,4,128]{3,2,1,0:T(4,128)S(1)} %all_gather.3.dir_ref, bf16[5,64,64,128]{3,2,1,0:T(8,128)(2,1)} %bitcast.36, f32[64,64]{1,0:T(8,128)S(1)} %bitcast.35), custom_call_target="tpu_custom_call" | custom-call | flops 200000000 | bytes 8000000 | tf_op jit(solution)/shard_map/adjoint/pallas_call | solution.py:153
  27.4 13.6 %all-to-all-start = ((f32[64,64,128]{2,1,0:T(8,128)}), f32[64,64,128]{2,1,0:T(8,128)S(1)}, u32[]{:S(2)}, u32[]{:S(2)}) async-start(f32[64,64,128]{2,1,0:T(8,128)} %adjoint.1), calls=%async_computation | async-start | bytes 4194304 | tf_op jit(solution)/shard_map/all_to_all | solution.py:182
  41.0 5.5 %reshape.28 = f32[64,2,64,2]{3,2,1,0:T(8,128)} reshape(f32[128,128]{1,0:T(8,128)S(1)} %copy-done.3) | data formatting | bytes 131072 | tf_op jit(solution)/shard_map/reshape | solution.py:166
  46.5 3.0 %copy.15 = f32[2,64,2,64]{3,2,1,0:T(2,128)S(1)} copy(f32[2,64,2,64]{2,3,0,1:T(8,128)} %bitcast.38) | data formatting | bytes 131072 | tf_op jit(solution)/shard_map/transpose | solution.py:166
  49.6 0.1 reshape.29.smooth_y_ref
  49.7 0.6 dynamic_slice.3.scale_ref
  50.3 3.3 %prepare.1 = (bf16[128,384]{1,0:T(8,128)(2,1)S(1)}, bf16[256,256]{1,0:T(8,128)(2,1)S(1)}, bf16[256,256]{1,0:T(8,128)(2,1)S(1)}) custom-call(s32[1]{0:T(128)} %dynamic_slice.3.scale_ref, f32[128,128]{1,0:T(8,128)S(1)} %reshape.29.smooth_y_ref, f32[256,256]{1,0:T(8,128)S(1)} %copy-done.1), custom_call_target="tpu_custom_call" | custom-call | flops 1000000000 | bytes 1000000 | tf_op jit(solution)/shard_map/prepare/pallas_call | solution.py:168
  53.6 84.4 %all-to-all-done.in_ref = f32[64,64,128]{2,1,0:T(8,128)S(1)} async-done(((f32[64,64,128]{2,1,0:T(8,128)}), f32[64,64,128]{2,1,0:T(8,128)S(1)}, u32[]{:S(2)}, u32[]{:S(2)}) %all-to-all-start) | async-done | bytes 2097184 | tf_op jit(solution)/shard_map/all_to_all | solution.py:182
  138.0 1.3 copy-done.2
  139.3 6.8 %smooth.1 = f32[64,64,128]{2,1,0:T(8,128)} custom-call(f32[64,64,128]{2,1,0:T(8,128)} %copy-done.2, bf16[128,384]{1,0:T(8,128)(2,1)S(1)} %get-tuple-element.10.y_ref, bf16[256,256]{1,0:T(8,128)(2,1)S(1)} %get-tuple-element.11.xh_ref, bf16[256,256]{1,0:T(8,128)(2,1)S(1)} %get-tuple-element.12.xl_ref), custom_call_target="tpu_custom_call" | custom-call | flops 1200000000 | bytes 4000000 | tf_op jit(solution)/shard_map/smooth/pallas_call | solution.py:183
  146.2 8.7 %all-to-all-start.1 = ((f32[64,64,128]{2,1,0:T(8,128)}), f32[64,64,128]{2,1,0:T(8,128)S(1)}, u32[]{:S(2)}, u32[]{:S(2)}) async-start(f32[64,64,128]{2,1,0:T(8,128)} %smooth.1), calls=%async_computation.1 | async-start | bytes 4194304 | tf_op jit(solution)/shard_map/all_to_all | solution.py:194
  154.9 0.1 pad_add_fusion.place_ref
  154.9 94.7 %all-to-all-done.1.in_ref = f32[64,64,128]{2,1,0:T(8,128)S(1)} async-done(((f32[64,64,128]{2,1,0:T(8,128)}), f32[64,64,128]{2,1,0:T(8,128)S(1)}, u32[]{:S(2)}, u32[]{:S(2)}) %all-to-all-start.1) | async-done | bytes 2097184 | tf_op jit(solution)/shard_map/all_to_all | solution.py:194
  249.6 5.8 %increment.1 = (f32[4,5,8,4,128]{4,3,2,1,0:T(4,128)S(1)}, f32[4,5,8,4,128]{4,3,2,1,0:T(4,128)S(1)}) custom-call(s32[2]{0:T(128)S(1)} %pad_add_fusion.place_ref, f32[64,64,128]{2,1,0:T(8,128)S(1)} %all-to-all-done.1.in_ref, bf16[5,64,64,128]{3,2,1,0:T(8,128)(2,1)} %bitcast.37, f32[64,64]{1,0:T(8,128)S(1)} %copy-done), custom_call_target="tpu_custom_call" | custom-call | flops 200000000 | bytes 8000000 | tf_op jit(solution)/shard_map/increment/pallas_call | solution.py:197
  255.4 8.3 %collective-permute-start = (f32[4,5,8,4,128]{4,3,2,1,0:T(4,128)S(1)}, f32[4,5,8,4,128]{4,3,2,1,0:T(4,128)S(1)}, u32[]{:S(2)}, u32[]{:S(2)}) collective-permute-start(f32[4,5,8,4,128]{4,3,2,1,0:T(4,128)S(1)} %get-tuple-element.14), channel_id=1, source_target_pairs={{0,1},{1,0},{2,3},{3,2},{4,5},{5,4},{6,7},{7,6},{8,9},{9,8},{10,11... | collective-permute-start | bytes 983048 | tf_op jit(solution)/shard_map/ppermute | solution.py:209
  263.8 1.2 collective-permute-done
  265.0 0.1 fusion.2
  265.1 3.1 %collective-permute-start.1 = (f32[5,8,4,128]{3,2,1,0:T(4,128)S(1)}, f32[5,8,4,128]{3,2,1,0:T(4,128)S(1)}, u32[]{:S(2)}, u32[]{:S(2)}) collective-permute-start(f32[5,8,4,128]{3,2,1,0:T(4,128)S(1)} %get-tuple-element.15), channel_id=1, source_target_pairs={{0,4},{1,5},{2,6},{3,7},{4,0},{5,1},{6,2},{7,3},{8,12},{9,13},{10,... | collective-permute-start | bytes 245768 | tf_op jit(solution)/shard_map/ppermute | solution.py:213
  268.2 3.4 %collective-permute-start.2 = (f32[5,8,4,128]{3,2,1,0:T(4,128)S(1)}, f32[5,8,4,128]{3,2,1,0:T(4,128)S(1)}, u32[]{:S(2)}, u32[]{:S(2)}) collective-permute-start(f32[5,8,4,128]{3,2,1,0:T(4,128)S(1)} %get-tuple-element.17), channel_id=1, source_target_pairs={{0,2},{1,3},{2,4},{3,5},{4,6},{5,7},{6,0},{7,1},{8,10},{9,11},{10,... | collective-permute-start | bytes 245768 | tf_op jit(solution)/shard_map/ppermute | solution.py:213
  271.6 3.1 %collective-permute-start.3 = (f32[5,8,4,128]{3,2,1,0:T(4,128)S(1)}, f32[5,8,4,128]{3,2,1,0:T(4,128)S(1)}, u32[]{:S(2)}, u32[]{:S(2)}) collective-permute-start(f32[5,8,4,128]{3,2,1,0:T(4,128)S(1)} %get-tuple-element.16), channel_id=1, source_target_pairs={{0,6},{1,7},{2,0},{3,1},{4,2},{5,3},{6,4},{7,5},{8,14},{9,15},{10,... | collective-permute-start | bytes 245768 | tf_op jit(solution)/shard_map/ppermute | solution.py:213
  274.7 2.1 collective-permute-done.3
  276.8 0.7 fusion.7
  (11 shorter events, 0.0 us)
Async XLA Ops:
  27.4 13.6 %copy-start.3 = (f32[128,128]{1,0:T(8,128)S(1)}, f32[128,128]{1,0:T(8,128)}, u32[]{:S(2)}) copy-start(f32[128,128]{1,0:T(8,128)} %param.8) | copy-start | bytes 196612
  27.4 110.6 %all-to-all-start = ((f32[64,64,128]{2,1,0:T(8,128)}), f32[64,64,128]{2,1,0:T(8,128)S(1)}, u32[]{:S(2)}, u32[]{:S(2)}) async-start(f32[64,64,128]{2,1,0:T(8,128)} %adjoint.1), calls=%async_computation | async-start | bytes 4194304 | tf_op jit(solution)/shard_map/all_to_all | solution.py:182
  46.5 3.2 %copy-start.4 = (s32[64]{0:T(128)S(1)}, s32[64]{0:T(128)}, u32[]{:S(2)}) copy-start(s32[64]{0:T(128)} %param.11) | copy-start | bytes 772
  46.5 3.8 %copy-start.1 = (f32[256,256]{1,0:T(8,128)S(1)}, f32[256,256]{1,0:T(8,128)}, u32[]{:S(2)}) copy-start(f32[256,256]{1,0:T(8,128)} %smooth_x_ref.1) | copy-start | bytes 786436
  138.0 1.3 copy-start.2
  146.1 103.4 %copy-start = (f32[64,64]{1,0:T(8,128)S(1)}, f32[64,64]{1,0:T(8,128)}, u32[]{:S(2)}) copy-start(f32[64,64]{1,0:T(8,128)} %matrix_ref.1) | copy-start | bytes 49156
  146.2 103.4 %all-to-all-start.1 = ((f32[64,64,128]{2,1,0:T(8,128)}), f32[64,64,128]{2,1,0:T(8,128)S(1)}, u32[]{:S(2)}, u32[]{:S(2)}) async-start(f32[64,64,128]{2,1,0:T(8,128)} %smooth.1), calls=%async_computation.1 | async-start | bytes 4194304 | tf_op jit(solution)/shard_map/all_to_all | solution.py:194
  255.4 9.6 %collective-permute-start = (f32[4,5,8,4,128]{4,3,2,1,0:T(4,128)S(1)}, f32[4,5,8,4,128]{4,3,2,1,0:T(4,128)S(1)}, u32[]{:S(2)}, u32[]{:S(2)}) collective-permute-start(f32[4,5,8,4,128]{4,3,2,1,0:T(4,128)S(1)} %get-tuple-element.14), channel_id=1, source_target_pairs={{0,1},{1,0},{2,3},{3,2},{4,5},{5,4},{6,7},{7,6},{8,9},{9,8},{10,11... | collective-permute-start | bytes 983048 | tf_op jit(solution)/shard_map/ppermute | solution.py:209
  265.1 9.6 %collective-permute-start.1 = (f32[5,8,4,128]{3,2,1,0:T(4,128)S(1)}, f32[5,8,4,128]{3,2,1,0:T(4,128)S(1)}, u32[]{:S(2)}, u32[]{:S(2)}) collective-permute-start(f32[5,8,4,128]{3,2,1,0:T(4,128)S(1)} %get-tuple-element.15), channel_id=1, source_target_pairs={{0,4},{1,5},{2,6},{3,7},{4,0},{5,1},{6,2},{7,3},{8,12},{9,13},{10,... | collective-permute-start | bytes 245768 | tf_op jit(solution)/shard_map/ppermute | solution.py:213
  268.2 6.5 %collective-permute-start.2 = (f32[5,8,4,128]{3,2,1,0:T(4,128)S(1)}, f32[5,8,4,128]{3,2,1,0:T(4,128)S(1)}, u32[]{:S(2)}, u32[]{:S(2)}) collective-permute-start(f32[5,8,4,128]{3,2,1,0:T(4,128)S(1)} %get-tuple-element.17), channel_id=1, source_target_pairs={{0,2},{1,3},{2,4},{3,5},{4,6},{5,7},{6,0},{7,1},{8,10},{9,11},{10,... | collective-permute-start | bytes 245768 | tf_op jit(solution)/shard_map/ppermute | solution.py:213
  271.6 5.2 %collective-permute-start.3 = (f32[5,8,4,128]{3,2,1,0:T(4,128)S(1)}, f32[5,8,4,128]{3,2,1,0:T(4,128)S(1)}, u32[]{:S(2)}, u32[]{:S(2)}) collective-permute-start(f32[5,8,4,128]{3,2,1,0:T(4,128)S(1)} %get-tuple-element.16), channel_id=1, source_target_pairs={{0,6},{1,7},{2,0},{3,1},{4,2},{5,3},{6,4},{7,5},{8,14},{9,15},{10,... | collective-permute-start | bytes 245768 | tf_op jit(solution)/shard_map/ppermute | solution.py:213

commit v2 on v0

v2 whole, which is shorter than its diff:
```python
import jax
import jax.numpy as jnp
from jax import lax
from jax.experimental import pallas as pl
from jax.experimental.pallas import tpu as pltpu
from jax.sharding import PartitionSpec as P

F32 = jnp.float32
BF16 = jnp.bfloat16
LEVELS = 64
VARS = 5
ROWS = 64
PITCH = 72
GROUP = 8


def split(value):
    high = value.astype(BF16)
    low = (value - high.astype(F32)).astype(BF16)
    return high, low


def dot(a, b):
    return jnp.dot(a, b, preferred_element_type=F32)


def every_level(row):
    return pl.ds(row, LEVELS, stride=PITCH)


def level_rows(level):
    return pl.ds(pl.multiple_of(level * PITCH, 8), ROWS)


def spread(source, target):
    for level in range(LEVELS):
        target[level * PITCH : level * PITCH + ROWS, :] = source[level * ROWS : (level + 1) * ROWS, :]


def vertical_product(matrix, source, target, after=lambda step: None):
    m_high, m_low = split(matrix)
    zero = jnp.zeros_like(m_high)
    left = jnp.concatenate(
        [jnp.concatenate([m_high, m_high], axis=1), jnp.concatenate([m_low, zero], axis=1)], axis=0
    )

    def half(step, carry):
        for pair in range(ROWS // 4):
            first = step * (ROWS // 2) + 2 * pair
            parts = [source[every_level(first + i), :] for i in range(2)]
            high, low = split(jnp.concatenate(parts, axis=1))
            result = dot(left, jnp.concatenate([high, low], axis=0))
            result = result[:LEVELS] + result[LEVELS:]
            for i in range(2):
                target[every_level(first + i), :] = result[:, 128 * i : 128 * (i + 1)]
            if pair % (GROUP // 2) == GROUP // 2 - 1:
                after(step * (ROWS // 2 // GROUP) + pair // (GROUP // 2))
        return carry

    lax.fori_loop(0, 2, half, 0)


def send_rows(result, out_ref, sem, step):
    rows = pl.ds(pl.multiple_of(step * GROUP, GROUP), GROUP)
    view = result.reshape(LEVELS, PITCH, 128)
    return pltpu.make_async_copy(view.at[:, rows], out_ref.at[:, rows], sem.at[step])


def wait_rows(result, out_ref, sem):
    for step in range(ROWS // GROUP):
        send_rows(result, out_ref, sem, step).wait()


def adjoint_kernel(dir_ref, perturb_ref, matrix_ref, out_ref, lines, controls, result, in_sem, out_sem):
    pieces = []
    for c in range(8):
        part = pl.ds(8 * c, 8)
        pieces.append(pltpu.make_async_copy(perturb_ref.at[:, part], lines.at[:, part], in_sem.at[c]))
        pieces[c].start()

    def level(q, carry):
        total = None
        for v in range(VARS):
            direction = dir_ref[v, q]
            direction = jnp.concatenate([direction, direction], axis=0)
            term = lines[v, q].astype(F32).reshape(ROWS // 8, 8, 128) * direction[None]
            total = term if total is None else total + term
        controls[level_rows(q), :] = total.reshape(ROWS, 128)
        return carry

    for c in range(8):
        pieces[c].wait()
        lax.fori_loop(8 * c, 8 * c + 8, level, 0, unroll=2)
    vertical_product(
        matrix_ref[...].T, controls, result, lambda step: send_rows(result, out_ref, out_sem, step).start()
    )
    wait_rows(result, out_ref, out_sem)


def prepare_kernel(scale_ref, smooth_y_ref, smooth_x_ref, y_ref, xh_ref, xl_ref):
    scale = scale_ref[0]

    def covariance(matrix):
        power = matrix
        chosen = matrix
        for step in range(2, 5):
            power = jnp.dot(matrix, power, precision=lax.Precision.HIGHEST, preferred_element_type=F32)
            chosen = jnp.where(scale == step, power, chosen)
        return lax.dot_general(
            chosen, chosen, (((1,), (1,)), ((), ())), precision=lax.Precision.HIGHEST, preferred_element_type=F32
        )

    high, low = split(covariance(smooth_y_ref[...]))
    y_ref[...] = jnp.concatenate([high, high, low], axis=1)
    high, low = split(covariance(smooth_x_ref[...]))
    xh_ref[...] = high
    xl_ref[...] = low


def smooth_kernel(in_ref, y_ref, xh_ref, xl_ref, out_ref, source, result, out_sem):
    xh, xl = xh_ref[...], xl_ref[...]
    y_both, y_low = y_ref[:, :256], y_ref[:, 256:]
    spread(in_ref, source)

    def member(k):
        halves = []
        for r in range(2):
            parts = [source[every_level(4 * k + 2 * half + r), :] for half in range(2)]
            halves.append(jnp.concatenate(parts, axis=1))
        high, low = split(jnp.concatenate(halves, axis=0))
        along_x = dot(high, xh) + dot(low, xh) + dot(high, xl)
        high, low = split(along_x)
        smoothed = dot(y_both, jnp.concatenate([high, low], axis=0)) + dot(y_low, high)
        for r in range(2):
            for half in range(2):
                result[every_level(4 * k + 2 * half + r), :] = smoothed[
                    64 * r : 64 * (r + 1), 128 * half : 128 * (half + 1)
                ]

    def group(step, carry):
        for k in range(4):
            member(step * 4 + k)
            if k % 2:
                send_rows(result, out_ref, out_sem, step * 2 + k // 2).start()
        return carry

    lax.fori_loop(0, 4, group, 0)
    wait_rows(result, out_ref, out_sem)


def fetch_levels(parity, perturb_ref, lines, sem):
    pieces = []
    for chip in range(4):
        part = pl.ds(chip * 16 + parity * 8, 8)
        pieces.append(pltpu.make_async_copy(perturb_ref.at[:, part], lines.at[chip], sem.at[chip]))
        pieces[chip].start()
    return pieces


def increment_terms(parity, pieces, lines, forward_ref, out_ref):
    for chip in range(4):
        pieces[chip].wait()

        def level(i, carry, chip=chip):
            field = forward_ref[level_rows(chip * 16 + parity * 8 + i), :]
            for v in range(VARS):
                terms = lines[chip, v, i].astype(F32) * field
                eight = jnp.sum(terms.reshape(ROWS // 8, 8, 128), axis=0)
                out_ref[chip, v, i] = eight[:4] + eight[4:]
            return carry

        lax.fori_loop(0, 8, level, 0, unroll=2)


def give_kernel(core_ref, in_ref, perturb_ref, matrix_ref, forward_ref, give_ref, lines, source, sem):
    parity = 1 - core_ref[0]
    pieces = fetch_levels(parity, perturb_ref, lines, sem)
    spread(in_ref, source)
    vertical_product(matrix_ref[...], source, forward_ref)
    increment_terms(parity, pieces, lines, forward_ref, give_ref)


def keep_kernel(core_ref, forward_ref, perturb_ref, keep_ref, lines, sem):
    parity = core_ref[0]
    pieces = fetch_levels(parity, perturb_ref, lines, sem)
    increment_terms(parity, pieces, lines, forward_ref, keep_ref)


def finish_kernel(in_ref, out_ref):
    total = (in_ref[0] + in_ref[1]) + (in_ref[2] + in_ref[3])
    out_ref[...] = total / (128 - 1)


VMEM = pl.BlockSpec(memory_space=pltpu.VMEM)
SMEM = pl.BlockSpec(memory_space=pltpu.SMEM)
HBM = pl.BlockSpec(memory_space=pltpu.HBM)
FIELDS = jax.ShapeDtypeStruct((LEVELS, ROWS, 128), F32)
FLAT = jax.ShapeDtypeStruct((LEVELS * ROWS, 128), F32)
SHARE = jax.ShapeDtypeStruct((4, VARS, 8, 4, 128), F32)
SPREAD = jax.ShapeDtypeStruct((LEVELS * PITCH, 128), F32)
SPREAD_SCRATCH = pltpu.VMEM(SPREAD.shape, F32)
HALF_SCRATCH = pltpu.VMEM((4, VARS, 8, ROWS, 128), BF16)
DMA = pltpu.SemaphoreType.DMA


def call(kernel, name, in_specs, out, flops, scratch=(), vmem=24):
    return pl.pallas_call(
        kernel,
        in_specs=in_specs,
        out_specs=[spec for spec, shape in out] if len(out) > 1 else out[0][0],
        out_shape=[shape for spec, shape in out] if len(out) > 1 else out[0][1],
        scratch_shapes=list(scratch),
        compiler_params=pltpu.CompilerParams(vmem_limit_bytes=vmem * 1024 * 1024),
        cost_estimate=pl.CostEstimate(flops=flops, bytes_accessed=4_000_000, transcendentals=0),
        name=name,
    )


adjoint_call = call(
    adjoint_kernel,
    "adjoint",
    [VMEM, HBM, VMEM],
    [(HBM, FIELDS)],
    300_000_000,
    [pltpu.VMEM((VARS, LEVELS, ROWS, 128), BF16), SPREAD_SCRATCH, SPREAD_SCRATCH, DMA((8,)), DMA((8,))],
    vmem=60,
)
prepare_call = call(
    prepare_kernel,
    "prepare",
    [SMEM, VMEM, VMEM],
    [
        (VMEM, jax.ShapeDtypeStruct((128, 384), BF16)),
        (VMEM, jax.ShapeDtypeStruct((256, 256), BF16)),
        (VMEM, jax.ShapeDtypeStruct((256, 256), BF16)),
    ],
    1_000_000_000,
)
smooth_call = call(
    smooth_kernel,
    "smooth",
    [VMEM] * 4,
    [(HBM, FIELDS)],
    1_200_000_000,
    [SPREAD_SCRATCH, SPREAD_SCRATCH, DMA((8,))],
    vmem=48,
)
give_call = call(
    give_kernel,
    "give",
    [SMEM, VMEM, HBM, VMEM],
    [(VMEM, SPREAD), (VMEM, SHARE)],
    300_000_000,
    [HALF_SCRATCH, SPREAD_SCRATCH, DMA((4,))],
    vmem=48,
)
keep_call = call(
    keep_kernel,
    "keep",
    [SMEM, VMEM, HBM],
    [(VMEM, SHARE)],
    100_000_000,
    [HALF_SCRATCH, DMA((4,))],
    vmem=48,
)
finish_call = call(
    finish_kernel, "finish", [VMEM], [(VMEM, jax.ShapeDtypeStruct((VARS, 8, 4, 128), F32))], 1_000_000
)


def to_lines(array):
    lead = array.shape[:-2]
    n = len(lead)
    array = array.reshape(lead + (2, 2, 128))
    return array.transpose(tuple(range(n)) + (n + 1, n, n + 2)).reshape(lead + (4, 128))


def exchange(fields):
    return lax.all_to_all(fields, "tile", split_axis=0, concat_axis=0, tiled=True)


def flat(fields):
    return fields.reshape(FLAT.shape)


def per_device(search_dir, perturb, smooth_y, smooth_x, vertical, level_scale):
    core = lax.rem(lax.axis_index("mem"), 2)[None]
    lines = to_lines(perturb).reshape(VARS, LEVELS, ROWS, 128)
    full_dir = lax.all_gather(to_lines(search_dir), "mem", axis=1, tiled=True)
    adjoint = adjoint_call(full_dir, lines, vertical)

    scale = lax.dynamic_slice_in_dim(level_scale, lax.axis_index("tile"), 1)
    ordered_y = smooth_y.reshape(64, 2, 64, 2).transpose(1, 0, 3, 2).reshape(128, 128)
    cov_y, cov_xh, cov_xl = prepare_call(scale, ordered_y, smooth_x)

    smoothed = smooth_call(flat(exchange(adjoint)), cov_y, cov_xh, cov_xl)
    forward, give = give_call(core, flat(exchange(smoothed)), lines, vertical)
    keep = keep_call(core, forward, lines)
    both = keep + lax.ppermute(give, "mem", [(m, m ^ 1) for m in range(8)])
    both = lax.all_to_all(
        both, "mem", split_axis=0, concat_axis=0, tiled=True, axis_index_groups=[[0, 2, 4, 6], [1, 3, 5, 7]]
    )
    total = finish_call(both).reshape(VARS, 8, 2, 2, 128).transpose(0, 1, 3, 2, 4)
    return total.reshape(VARS, 8, 2, 256)


def solution(mesh):
    in_specs = (
        P(None, "mem", "tile", None),
        P(None, None, "mem", "tile", None),
        P(),
        P(),
        P(),
        P(),
    )
    out_specs = P(None, "mem", "tile", None)
    return jax.shard_map(
        per_device, mesh=mesh, in_specs=in_specs, out_specs=out_specs, check_vma=False
    )
```

time: 339 us -> 272 us (0.80)
  waiting for transfers between devices: 76.5 us -> 179 us
  blocking collectives: 123 us -> 31.4 us
  other arithmetic: 63.7 us -> 0.09 us
  Pallas kernels: 0 us -> 19.8 us
  matrix products: 19.1 us -> 0 us
  starting transfers between devices: 13.8 us -> 30.6 us
  local copies, waits for them, and re-layouts: 26.8 us -> 10.6 us
  between operations: 13.7 us -> 0.13 us
    all_to_all x1 -> x2, waiting for transfers between devices: 42.4 us -> 179 us  [exchange(): lax.all_to_all(fields, 'tile', split_axis=0, concat_axis=0, tiled=True)]
    all_to_all x1, blocking collectives: 103 us -> 10.1 us  [per_device(): lax.all_to_all(both, 'mem', split_axis=0, concat_axis=0, tiled=True, axis...]
    select_n x1 -> x0, other arithmetic: 35.6 us -> none  [per_device(): jnp.repeat(level_scale, members, total_repeat_length=levels * members)]
    unnamed x2 -> x0, waiting for transfers between devices: 34.1 us -> none
    reduce_sum x2 -> x0, other arithmetic: 22.1 us -> none  [the longest x1 13.1 us: per_device(): jnp.sum(perturb.astype(jnp.float32) * full_dir[:, :, None], axis=0)]
    pallas_call x0 -> x6, Pallas kernels: none -> 19.8 us  [the longest x1 6.34 us: per_device(): smoothed = smooth_call(flat(exchange(adjoint)), cov_y, cov_xh, cov_xl)]
    dot_general x20 -> x0, matrix products: 19.1 us -> none  [the longest x1 3.59 us: per_device(): forward = jnp.dot(vertical, returned.reshape(levels, -1), precision=highest)]
    all_to_all x1 -> x2, starting transfers between devices: 13.6 us -> 22.2 us  [exchange(): lax.all_to_all(fields, 'tile', split_axis=0, concat_axis=0, tiled=True)]
  transfers between devices with their start and end apart: 2 -> 3, of which waited for: 2 -> 2; matrix products, arithmetic and copies ran while one was open for 16% -> 3% of each run, Pallas kernels for 0% -> 2%
where the time goes in v2:
time: 272 us
  waiting for transfers between devices  179 us (66%)
  blocking collectives  31.4 us (12%)
  starting transfers between devices  30.6 us (11%)
  Pallas kernels  19.8 us (7%)
  local copies, waits for them, and re-layouts  10.6 us (4%)
    all_to_all x2, waiting for transfers between devices, exchange(): lax.all_to_all(fields, 'tile', split_axis=0, concat_axis=0, tiled=True)  179 us
    all_to_all x2, starting transfers between devices, exchange(): lax.all_to_all(fields, 'tile', split_axis=0, concat_axis=0, tiled=True)  22.2 us
    all_gather x1, blocking collectives, per_device(): full_dir = lax.all_gather(to_lines(search_dir), 'mem', axis=1, tiled=True)  21.3 us
    all_to_all x1, blocking collectives, per_device(): lax.all_to_all(both, 'mem', split_axis=0, concat_axis=0, tiled=True, axis...  10.1 us
    ppermute x1, starting transfers between devices, per_device(): both = keep + lax.ppermute(give, 'mem', [(m, m ^ 1) for m in range(8)])  8.34 us
    pallas_call x1, Pallas kernels, per_device(): smoothed = smooth_call(flat(exchange(adjoint)), cov_y, cov_xh, cov_xl)  6.34 us
    pallas_call x1, Pallas kernels, per_device(): adjoint = adjoint_call(full_dir, lines, vertical)  5.67 us
    reshape x2, local copies, waits for them, and re-layouts, per_device(): smooth_y.reshape(64, 2, 64, 2).transpose(1, 0, 3, 2).reshape(128, 128)  5.66 us
  transfers between devices with their start and end apart: 3, of which 2 were waited for; matrix products, arithmetic and copies ran while one was open for 3% of the time, Pallas kernels for 2%

profile of v2, /device:TPU:1, one launch (start us, length us, event | category | flops | bytes accessed | tf_op | source)
XLA Modules:
  0.0 271.7 jit_solution(11360737676384116448)
XLA Ops:
  0.0 21.3 %all_gather.3.dir_ref = f32[5,64,4,128]{3,2,1,0:T(4,128)} all-gather(f32[5,8,4,128]{3,2,1,0:T(4,128)} %bitcast.25), channel_id=1, replica_groups=mesh['tile'=64,'mem'=8] {'mem'}, dimensions={1}, use_global_device_ids=true | all-gather | bytes 737280 | tf_op jit(solution)/shard_map/all_gather | solution.py:289
  21.3 5.7 %adjoint.1 = f32[64,64,128]{2,1,0:T(8,128)} custom-call(f32[5,64,4,128]{3,2,1,0:T(4,128)} %all_gather.3.dir_ref, bf16[5,64,64,128]{3,2,1,0:T(8,128)(2,1)} %bitcast.21, f32[64,64]{1,0:T(8,128)} %matrix_ref.3), custom_call_target="tpu_custom_call" | custom-call | flops 300000000 | bytes 4000000 | tf_op jit(solution)/shard_map/adjoint/pallas_call | solution.py:290
  26.9 0.0 copy-start.3
  27.0 13.6 %all-to-all-start = ((f32[64,64,128]{2,1,0:T(8,128)}), f32[64,64,128]{2,1,0:T(8,128)S(1)}, u32[]{:S(2)}, u32[]{:S(2)}) async-start(f32[64,64,128]{2,1,0:T(8,128)} %adjoint.1), calls=%async_computation | async-start | bytes 4194304 | tf_op jit(solution)/shard_map/all_to_all | solution.py:279
  40.5 0.0 copy-done.3
  40.5 5.5 %reshape.31 = f32[64,2,64,2]{3,2,1,0:T(8,128)} reshape(f32[128,128]{1,0:T(8,128)S(1)} %copy-done.3) | data formatting | bytes 131072 | tf_op jit(solution)/shard_map/reshape | solution.py:293
  46.1 3.0 %copy.13 = f32[2,64,2,64]{3,2,1,0:T(2,128)S(1)} copy(f32[2,64,2,64]{2,3,0,1:T(8,128)} %bitcast.24) | data formatting | bytes 131072 | tf_op jit(solution)/shard_map/transpose | solution.py:293
  49.1 0.1 reshape.32.smooth_y_ref
  49.3 0.0 copy-done.4
  49.3 0.6 dynamic_slice.3.scale_ref
  49.8 0.0 copy-done.2
  49.8 3.3 %prepare.1 = (bf16[128,384]{1,0:T(8,128)(2,1)S(1)}, bf16[256,256]{1,0:T(8,128)(2,1)S(1)}, bf16[256,256]{1,0:T(8,128)(2,1)S(1)}) custom-call(s32[1]{0:T(128)} %dynamic_slice.3.scale_ref, f32[128,128]{1,0:T(8,128)S(1)} %reshape.32.smooth_y_ref, f32[256,256]{1,0:T(8,128)S(1)} %copy-done.2), custom_call_target="tpu_custom_call" | custom-call | flops 1000000000 | bytes 4000000 | tf_op jit(solution)/shard_map/prepare/pallas_call | solution.py:294
  53.2 84.4 %all-to-all-done = f32[64,64,128]{2,1,0:T(8,128)S(1)} async-done(((f32[64,64,128]{2,1,0:T(8,128)}), f32[64,64,128]{2,1,0:T(8,128)S(1)}, u32[]{:S(2)}, u32[]{:S(2)}) %all-to-all-start) | async-done | bytes 2097184 | tf_op jit(solution)/shard_map/all_to_all | solution.py:279
  137.6 6.3 %smooth.1 = f32[64,64,128]{2,1,0:T(8,128)S(1)} custom-call(f32[4096,128]{1,0:T(8,128)S(1)} %bitcast.19, bf16[128,384]{1,0:T(8,128)(2,1)S(1)} %get-tuple-element.10.y_ref, bf16[256,256]{1,0:T(8,128)(2,1)S(1)} %get-tuple-element.11.xh_ref, bf16[256,256]{1,0:T(8,128)(2,1)S(1)} %get-tuple-element.12.xl_ref), custom_call_target="tpu_custom_call" | custom-call | flops 1200000000 | bytes 4000000 | tf_op jit(solution)/shard_map/smooth/pallas_call | solution.py:296
  143.9 1.3 copy-done
  145.2 8.7 %all-to-all-start.1 = ((f32[64,64,128]{2,1,0:T(8,128)}), f32[64,64,128]{2,1,0:T(8,128)S(1)}, u32[]{:S(2)}, u32[]{:S(2)}) async-start(f32[64,64,128]{2,1,0:T(8,128)} %copy-done), calls=%async_computation.1 | async-start | bytes 4194304 | tf_op jit(solution)/shard_map/all_to_all | solution.py:279
  153.9 94.7 %all-to-all-done.1 = f32[64,64,128]{2,1,0:T(8,128)S(1)} async-done(((f32[64,64,128]{2,1,0:T(8,128)}), f32[64,64,128]{2,1,0:T(8,128)S(1)}, u32[]{:S(2)}, u32[]{:S(2)}) %all-to-all-start.1) | async-done | bytes 2097184 | tf_op jit(solution)/shard_map/all_to_all | solution.py:279
  248.7 1.9 give.1
  250.5 8.3 %collective-permute-start = (f32[4,5,8,4,128]{4,3,2,1,0:T(4,128)S(1)}, f32[4,5,8,4,128]{4,3,2,1,0:T(4,128)S(1)}, u32[]{:S(2)}, u32[]{:S(2)}) collective-permute-start(f32[4,5,8,4,128]{4,3,2,1,0:T(4,128)S(1)} %get-tuple-element.14), channel_id=1, source_target_pairs={{0,1},{1,0},{2,3},{3,2},{4,5},{5,4},{6,7},{7,6},{8,9},{9,8},{10,11... | collective-permute-start | bytes 983048 | tf_op jit(solution)/shard_map/ppermute | solution.py:299
  258.9 1.9 keep.1
  260.8 0.0 collective-permute-done
  260.8 0.1 add.7
  260.9 10.1 %all_to_all.15.in_ref = f32[4,5,8,4,128]{4,3,2,1,0:T(4,128)S(1)} all-to-all(f32[4,5,8,4,128]{4,3,2,1,0:T(4,128)S(1)} %add.7), channel_id=1, replica_groups={{0,2,4,6},{1,3,5,7},{8,10,12,14},{9,11,13,15},{16,18,20,22},{17,19,21,2..., dimensions={0} | all-to-all | bytes 655360 | tf_op jit(solution)/shard_map/all_to_all | solution.py:300
  271.0 0.7 finish.1
  (5 shorter events, 0.0 us)
Async XLA Ops:
  26.9 13.6 %copy-start.3 = (f32[128,128]{1,0:T(8,128)S(1)}, f32[128,128]{1,0:T(8,128)}, u32[]{:S(2)}) copy-start(f32[128,128]{1,0:T(8,128)} %param.8) | copy-start | bytes 196612
  27.0 110.6 %all-to-all-start = ((f32[64,64,128]{2,1,0:T(8,128)}), f32[64,64,128]{2,1,0:T(8,128)S(1)}, u32[]{:S(2)}, u32[]{:S(2)}) async-start(f32[64,64,128]{2,1,0:T(8,128)} %adjoint.1), calls=%async_computation | async-start | bytes 4194304 | tf_op jit(solution)/shard_map/all_to_all | solution.py:279
  46.1 3.2 %copy-start.4 = (s32[64]{0:T(128)S(1)}, s32[64]{0:T(128)}, u32[]{:S(2)}) copy-start(s32[64]{0:T(128)} %param.11) | copy-start | bytes 772
  46.1 3.8 %copy-start.2 = (f32[256,256]{1,0:T(8,128)S(1)}, f32[256,256]{1,0:T(8,128)}, u32[]{:S(2)}) copy-start(f32[256,256]{1,0:T(8,128)} %smooth_x_ref.1) | copy-start | bytes 786436
  143.9 1.3 copy-start
  145.2 103.4 %copy-start.1 = (f32[64,64]{1,0:T(8,128)S(1)}, f32[64,64]{1,0:T(8,128)}, u32[]{:S(2)}) copy-start(f32[64,64]{1,0:T(8,128)} %matrix_ref.3) | copy-start | bytes 49156
  145.2 103.4 %all-to-all-start.1 = ((f32[64,64,128]{2,1,0:T(8,128)}), f32[64,64,128]{2,1,0:T(8,128)S(1)}, u32[]{:S(2)}, u32[]{:S(2)}) async-start(f32[64,64,128]{2,1,0:T(8,128)} %copy-done), calls=%async_computation.1 | async-start | bytes 4194304 | tf_op jit(solution)/shard_map/all_to_all | solution.py:279
  250.5 10.2 %collective-permute-start = (f32[4,5,8,4,128]{4,3,2,1,0:T(4,128)S(1)}, f32[4,5,8,4,128]{4,3,2,1,0:T(4,128)S(1)}, u32[]{:S(2)}, u32[]{:S(2)}) collective-permute-start(f32[4,5,8,4,128]{4,3,2,1,0:T(4,128)S(1)} %get-tuple-element.14), channel_id=1, source_target_pairs={{0,1},{1,0},{2,3},{3,2},{4,5},{5,4},{6,7},{7,6},{8,9},{9,8},{10,11... | collective-permute-start | bytes 983048 | tf_op jit(solution)/shard_map/ppermute | solution.py:299

commit v3 on v2

--- a/solution.py
+++ b/solution.py
@@ -12,6 +12,7 @@
 ROWS = 64
 PITCH = 72
 GROUP = 8
+MEMBERS_AT_ONCE = 4
 
 
 def split(value):
@@ -60,15 +61,15 @@
     lax.fori_loop(0, 2, half, 0)
 
 
-def send_rows(result, out_ref, sem, step):
-    rows = pl.ds(pl.multiple_of(step * GROUP, GROUP), GROUP)
+def send_rows(result, out_ref, sem, step, count=GROUP):
+    rows = pl.ds(pl.multiple_of(step * count, GROUP), count)
     view = result.reshape(LEVELS, PITCH, 128)
     return pltpu.make_async_copy(view.at[:, rows], out_ref.at[:, rows], sem.at[step])
 
 
-def wait_rows(result, out_ref, sem):
-    for step in range(ROWS // GROUP):
-        send_rows(result, out_ref, sem, step).wait()
+def wait_rows(result, out_ref, sem, count=GROUP):
+    for step in range(ROWS // count):
+        send_rows(result, out_ref, sem, step, count).wait()
 
 
 def adjoint_kernel(dir_ref, perturb_ref, matrix_ref, out_ref, lines, controls, result, in_sem, out_sem):
@@ -117,35 +118,30 @@
     xl_ref[...] = low
 
 
-def smooth_kernel(in_ref, y_ref, xh_ref, xl_ref, out_ref, source, result, out_sem):
+def smooth_kernel(in_ref, y_ref, xh_ref, xl_ref, spent_ref, out_ref, source, result, out_sem):
+    del spent_ref
     xh, xl = xh_ref[...], xl_ref[...]
     y_both, y_low = y_ref[:, :256], y_ref[:, 256:]
     spread(in_ref, source)
-
-    def member(k):
+    for step in range(ROWS // 4 // MEMBERS_AT_ONCE):
+        first = step * MEMBERS_AT_ONCE * 4
         halves = []
-        for r in range(2):
-            parts = [source[every_level(4 * k + 2 * half + r), :] for half in range(2)]
-            halves.append(jnp.concatenate(parts, axis=1))
+        for k in range(MEMBERS_AT_ONCE):
+            for r in range(2):
+                parts = [source[every_level(first + 4 * k + 2 * half + r), :] for half in range(2)]
+                halves.append(jnp.concatenate(parts, axis=1))
         high, low = split(jnp.concatenate(halves, axis=0))
         along_x = dot(high, xh) + dot(low, xh) + dot(high, xl)
-        high, low = split(along_x)
-        smoothed = dot(y_both, jnp.concatenate([high, low], axis=0)) + dot(y_low, high)
-        for r in range(2):
-            for half in range(2):
-                result[every_level(4 * k + 2 * half + r), :] = smoothed[
-                    64 * r : 64 * (r + 1), 128 * half : 128 * (half + 1)
-                ]
-
-    def group(step, carry):
-        for k in range(4):
-            member(step * 4 + k)
-            if k % 2:
-                send_rows(result, out_ref, out_sem, step * 2 + k // 2).start()
-        return carry
-
-    lax.fori_loop(0, 4, group, 0)
-    wait_rows(result, out_ref, out_sem)
+        for k in range(MEMBERS_AT_ONCE):
+            high, low = split(along_x[128 * k : 128 * (k + 1)])
+            smoothed = dot(y_both, jnp.concatenate([high, low], axis=0)) + dot(y_low, high)
+            for r in range(2):
+                for half in range(2):
+                    result[every_level(first + 4 * k + 2 * half + r), :] = smoothed[
+                        64 * r : 64 * (r + 1), 128 * half : 128 * (half + 1)
+                    ]
+        send_rows(result, out_ref, out_sem, step, 4 * MEMBERS_AT_ONCE).start()
+    wait_rows(result, out_ref, out_sem, 4 * MEMBERS_AT_ONCE)
 
 
 def fetch_levels(parity, perturb_ref, lines, sem):
@@ -203,13 +199,14 @@
 DMA = pltpu.SemaphoreType.DMA
 
 
-def call(kernel, name, in_specs, out, flops, scratch=(), vmem=24):
+def call(kernel, name, in_specs, out, flops, scratch=(), vmem=24, aliases=None):
     return pl.pallas_call(
         kernel,
         in_specs=in_specs,
         out_specs=[spec for spec, shape in out] if len(out) > 1 else out[0][0],
         out_shape=[shape for spec, shape in out] if len(out) > 1 else out[0][1],
         scratch_shapes=list(scratch),
+        input_output_aliases=aliases or {},
         compiler_params=pltpu.CompilerParams(vmem_limit_bytes=vmem * 1024 * 1024),
         cost_estimate=pl.CostEstimate(flops=flops, bytes_accessed=4_000_000, transcendentals=0),
         name=name,
@@ -239,11 +236,12 @@
 smooth_call = call(
     smooth_kernel,
     "smooth",
-    [VMEM] * 4,
+    [VMEM] * 4 + [HBM],
     [(HBM, FIELDS)],
     1_200_000_000,
-    [SPREAD_SCRATCH, SPREAD_SCRATCH, DMA((8,))],
+    [SPREAD_SCRATCH, SPREAD_SCRATCH, DMA((4,))],
     vmem=48,
+    aliases={4: 0},
 )
 give_call = call(
     give_kernel,
@@ -293,7 +291,7 @@
     ordered_y = smooth_y.reshape(64, 2, 64, 2).transpose(1, 0, 3, 2).reshape(128, 128)
     cov_y, cov_xh, cov_xl = prepare_call(scale, ordered_y, smooth_x)
 
-    smoothed = smooth_call(flat(exchange(adjoint)), cov_y, cov_xh, cov_xl)
+    smoothed = smooth_call(flat(exchange(adjoint)), cov_y, cov_xh, cov_xl, adjoint)
     forward, give = give_call(core, flat(exchange(smoothed)), lines, vertical)
     keep = keep_call(core, forward, lines)
     both = keep + lax.ppermute(give, "mem", [(m, m ^ 1) for m in range(8)])

time: 272 us -> 268 us (0.985)
  no operation moved by 1% of the time
where the time goes in v3:
time: 268 us
  waiting for transfers between devices  179 us (67%)
  blocking collectives  31.4 us (12%)
  starting transfers between devices  30.5 us (11%)
  Pallas kernels  17.1 us (6%)
  local copies, waits for them, and re-layouts  9.31 us (3%)
    all_to_all x2, waiting for transfers between devices, exchange(): lax.all_to_all(fields, 'tile', split_axis=0, concat_axis=0, tiled=True)  179 us
    all_to_all x2, starting transfers between devices, exchange(): lax.all_to_all(fields, 'tile', split_axis=0, concat_axis=0, tiled=True)  22.1 us
    all_gather x1, blocking collectives, per_device(): full_dir = lax.all_gather(to_lines(search_dir), 'mem', axis=1, tiled=True)  21.3 us
    all_to_all x1, blocking collectives, per_device(): lax.all_to_all(both, 'mem', split_axis=0, concat_axis=0, tiled=True, axis...  10.1 us
    ppermute x1, starting transfers between devices, per_device(): both = keep + lax.ppermute(give, 'mem', [(m, m ^ 1) for m in range(8)])  8.35 us
    pallas_call x1, Pallas kernels, per_device(): adjoint = adjoint_call(full_dir, lines, vertical)  5.71 us
    reshape x2, local copies, waits for them, and re-layouts, per_device(): smooth_y.reshape(64, 2, 64, 2).transpose(1, 0, 3, 2).reshape(128, 128)  5.66 us
  transfers between devices with their start and end apart: 3, of which 2 were waited for; matrix products, arithmetic and copies ran while one was open for 3% of the time, Pallas kernels for 2%

profile of v3, /device:TPU:1, one launch (start us, length us, event | category | flops | bytes accessed | tf_op | source)
XLA Modules:
  0.0 267.6 jit_solution(10202212918180271134)
XLA Ops:
  0.0 21.3 %all_gather.3.dir_ref = f32[5,64,4,128]{3,2,1,0:T(4,128)} all-gather(f32[5,8,4,128]{3,2,1,0:T(4,128)} %bitcast.25), channel_id=1, replica_groups=mesh['tile'=64,'mem'=8] {'mem'}, dimensions={1}, use_global_device_ids=true | all-gather | bytes 737280 | tf_op jit(solution)/shard_map/all_gather | solution.py:287
  21.3 5.7 %adjoint.1.spent_ref = f32[64,64,128]{2,1,0:T(8,128)} custom-call(f32[5,64,4,128]{3,2,1,0:T(4,128)} %all_gather.3.dir_ref, bf16[5,64,64,128]{3,2,1,0:T(8,128)(2,1)} %bitcast.21, f32[64,64]{1,0:T(8,128)} %matrix_ref.3), custom_call_target="tpu_custom_call" | custom-call | flops 300000000 | bytes 4000000 | tf_op jit(solution)/shard_map/adjoint/pallas_call | solution.py:288
  27.0 0.0 copy-start.2
  27.0 13.6 %all-to-all-start = ((f32[64,64,128]{2,1,0:T(8,128)}), f32[64,64,128]{2,1,0:T(8,128)S(1)}, u32[]{:S(2)}, u32[]{:S(2)}) async-start(f32[64,64,128]{2,1,0:T(8,128)} %adjoint.1.spent_ref), calls=%async_computation | async-start | bytes 4194304 | tf_op jit(solution)/shard_map/all_to_all | solution.py:277
  40.6 0.0 copy-done.2
  40.6 5.5 %reshape.31 = f32[64,2,64,2]{3,2,1,0:T(8,128)} reshape(f32[128,128]{1,0:T(8,128)S(1)} %copy-done.2) | data formatting | bytes 131072 | tf_op jit(solution)/shard_map/reshape | solution.py:291
  46.1 3.0 %copy.14 = f32[2,64,2,64]{3,2,1,0:T(2,128)S(1)} copy(f32[2,64,2,64]{2,3,0,1:T(8,128)} %bitcast.24) | data formatting | bytes 131072 | tf_op jit(solution)/shard_map/transpose | solution.py:291
  49.2 0.1 reshape.32.smooth_y_ref
  49.3 0.6 dynamic_slice.3.scale_ref
  49.9 0.0 copy-done.1
  49.9 3.3 %prepare.1 = (bf16[128,384]{1,0:T(8,128)(2,1)S(1)}, bf16[256,256]{1,0:T(8,128)(2,1)S(1)}, bf16[256,256]{1,0:T(8,128)(2,1)S(1)}) custom-call(s32[1]{0:T(128)} %dynamic_slice.3.scale_ref, f32[128,128]{1,0:T(8,128)S(1)} %reshape.32.smooth_y_ref, f32[256,256]{1,0:T(8,128)S(1)} %copy-done.1), custom_call_target="tpu_custom_call" | custom-call | flops 1000000000 | bytes 4000000 | tf_op jit(solution)/shard_map/prepare/pallas_call | solution.py:292
  53.2 84.4 %all-to-all-done = f32[64,64,128]{2,1,0:T(8,128)S(1)} async-done(((f32[64,64,128]{2,1,0:T(8,128)}), f32[64,64,128]{2,1,0:T(8,128)S(1)}, u32[]{:S(2)}, u32[]{:S(2)}) %all-to-all-start) | async-done | bytes 2097184 | tf_op jit(solution)/shard_map/all_to_all | solution.py:277
  137.6 3.6 %smooth.1 = f32[64,64,128]{2,1,0:T(8,128)} custom-call(f32[4096,128]{1,0:T(8,128)S(1)} %bitcast.19, bf16[128,384]{1,0:T(8,128)(2,1)S(1)} %get-tuple-element.10.y_ref, bf16[256,256]{1,0:T(8,128)(2,1)S(1)} %get-tuple-element.11.xh_ref, bf16[256,256]{1,0:T(8,128)(2,1)S(1)} %get-tuple-element.12.xl_ref, ...), custom_call_target="tpu_custom_call", output_to_operand_aliasing={{}: (4, {})} | custom-call | flops 1200000000 | bytes 4000000 | tf_op jit(solution)/shard_map/smooth/pallas_call | solution.py:294
  141.2 0.0 copy-start
  141.3 8.5 %all-to-all-start.1 = ((f32[64,64,128]{2,1,0:T(8,128)}), f32[64,64,128]{2,1,0:T(8,128)S(1)}, u32[]{:S(2)}, u32[]{:S(2)}) async-start(f32[64,64,128]{2,1,0:T(8,128)} %smooth.1), calls=%async_computation.1 | async-start | bytes 4194304 | tf_op jit(solution)/shard_map/all_to_all | solution.py:277
  149.8 94.7 %all-to-all-done.1 = f32[64,64,128]{2,1,0:T(8,128)S(1)} async-done(((f32[64,64,128]{2,1,0:T(8,128)}), f32[64,64,128]{2,1,0:T(8,128)S(1)}, u32[]{:S(2)}, u32[]{:S(2)}) %all-to-all-start.1) | async-done | bytes 2097184 | tf_op jit(solution)/shard_map/all_to_all | solution.py:277
  244.6 0.0 copy-done
  244.6 1.9 give.1
  246.4 8.3 %collective-permute-start = (f32[4,5,8,4,128]{4,3,2,1,0:T(4,128)S(1)}, f32[4,5,8,4,128]{4,3,2,1,0:T(4,128)S(1)}, u32[]{:S(2)}, u32[]{:S(2)}) collective-permute-start(f32[4,5,8,4,128]{4,3,2,1,0:T(4,128)S(1)} %get-tuple-element.14), channel_id=1, source_target_pairs={{0,1},{1,0},{2,3},{3,2},{4,5},{5,4},{6,7},{7,6},{8,9},{9,8},{10,11... | collective-permute-start | bytes 983048 | tf_op jit(solution)/shard_map/ppermute | solution.py:297
  254.8 1.9 keep.1
  256.7 0.0 collective-permute-done
  256.7 0.1 add.7
  256.8 10.1 %all_to_all.15.in_ref = f32[4,5,8,4,128]{4,3,2,1,0:T(4,128)S(1)} all-to-all(f32[4,5,8,4,128]{4,3,2,1,0:T(4,128)S(1)} %add.7), channel_id=1, replica_groups={{0,2,4,6},{1,3,5,7},{8,10,12,14},{9,11,13,15},{16,18,20,22},{17,19,21,2..., dimensions={0} | all-to-all | bytes 655360 | tf_op jit(solution)/shard_map/all_to_all | solution.py:298
  266.9 0.7 finish.1
  (3 shorter events, 0.0 us)
Async XLA Ops:
  27.0 13.6 %copy-start.2 = (f32[128,128]{1,0:T(8,128)S(1)}, f32[128,128]{1,0:T(8,128)}, u32[]{:S(2)}) copy-start(f32[128,128]{1,0:T(8,128)} %param.8) | copy-start | bytes 196612
  27.0 110.6 %all-to-all-start = ((f32[64,64,128]{2,1,0:T(8,128)}), f32[64,64,128]{2,1,0:T(8,128)S(1)}, u32[]{:S(2)}, u32[]{:S(2)}) async-start(f32[64,64,128]{2,1,0:T(8,128)} %adjoint.1.spent_ref), calls=%async_computation | async-start | bytes 4194304 | tf_op jit(solution)/shard_map/all_to_all | solution.py:277
  46.1 3.2 %copy-start.3 = (s32[64]{0:T(128)S(1)}, s32[64]{0:T(128)}, u32[]{:S(2)}) copy-start(s32[64]{0:T(128)} %param.11) | copy-start | bytes 772
  46.1 3.8 %copy-start.1 = (f32[256,256]{1,0:T(8,128)S(1)}, f32[256,256]{1,0:T(8,128)}, u32[]{:S(2)}) copy-start(f32[256,256]{1,0:T(8,128)} %smooth_x_ref.1) | copy-start | bytes 786436
  141.2 103.3 %copy-start = (f32[64,64]{1,0:T(8,128)S(1)}, f32[64,64]{1,0:T(8,128)}, u32[]{:S(2)}) copy-start(f32[64,64]{1,0:T(8,128)} %matrix_ref.3) | copy-start | bytes 49156
  141.3 103.3 %all-to-all-start.1 = ((f32[64,64,128]{2,1,0:T(8,128)}), f32[64,64,128]{2,1,0:T(8,128)S(1)}, u32[]{:S(2)}, u32[]{:S(2)}) async-start(f32[64,64,128]{2,1,0:T(8,128)} %smooth.1), calls=%async_computation.1 | async-start | bytes 4194304 | tf_op jit(solution)/shard_map/all_to_all | solution.py:277
  246.4 10.2 %collective-permute-start = (f32[4,5,8,4,128]{4,3,2,1,0:T(4,128)S(1)}, f32[4,5,8,4,128]{4,3,2,1,0:T(4,128)S(1)}, u32[]{:S(2)}, u32[]{:S(2)}) collective-permute-start(f32[4,5,8,4,128]{4,3,2,1,0:T(4,128)S(1)} %get-tuple-element.14), channel_id=1, source_target_pairs={{0,1},{1,0},{2,3},{3,2},{4,5},{5,4},{6,7},{7,6},{8,9},{9,8},{10,11... | collective-permute-start | bytes 983048 | tf_op jit(solution)/shard_map/ppermute | solution.py:297

commit v4 on v3

--- a/solution.py
+++ b/solution.py
@@ -13,6 +13,7 @@
 PITCH = 72
 GROUP = 8
 MEMBERS_AT_ONCE = 4
+WIDE_GROUP = 4 * MEMBERS_AT_ONCE
 
 
 def split(value):
@@ -25,6 +26,12 @@
     return jnp.dot(a, b, preferred_element_type=F32)
 
 
+def outer(matrix):
+    return lax.dot_general(
+        matrix, matrix, (((1,), (1,)), ((), ())), precision=lax.Precision.HIGHEST, preferred_element_type=F32
+    )
+
+
 def every_level(row):
     return pl.ds(row, LEVELS, stride=PITCH)
 
@@ -38,7 +45,7 @@
         target[level * PITCH : level * PITCH + ROWS, :] = source[level * ROWS : (level + 1) * ROWS, :]
 
 
-def vertical_product(matrix, source, target, after=lambda step: None):
+def vertical_product(matrix, source, target):
     m_high, m_low = split(matrix)
     zero = jnp.zeros_like(m_high)
     left = jnp.concatenate(
@@ -54,8 +61,6 @@
             result = result[:LEVELS] + result[LEVELS:]
             for i in range(2):
                 target[every_level(first + i), :] = result[:, 128 * i : 128 * (i + 1)]
-            if pair % (GROUP // 2) == GROUP // 2 - 1:
-                after(step * (ROWS // 2 // GROUP) + pair // (GROUP // 2))
         return carry
 
     lax.fori_loop(0, 2, half, 0)
@@ -72,7 +77,51 @@
         send_rows(result, out_ref, sem, step, count).wait()
 
 
-def adjoint_kernel(dir_ref, perturb_ref, matrix_ref, out_ref, lines, controls, result, in_sem, out_sem):
+def smooth_along_x(scale_ref, smooth_x_ref, fields, x_high, x_low):
+    matrix = smooth_x_ref[...]
+    power = matrix
+    for step in range(4):
+        if step:
+            power = jnp.dot(matrix, power, precision=lax.Precision.HIGHEST, preferred_element_type=F32)
+        high, low = split(outer(power))
+        x_high[step] = high
+        x_low[step] = low
+
+    def level(q, carry):
+        scale = scale_ref[q] - 1
+        places = [[pl.ds(q * PITCH + 2 * half + r, ROWS // 4, stride=4) for half in range(2)] for r in range(2)]
+        lines = [jnp.concatenate([fields[place, :] for place in pair], axis=1) for pair in places]
+        high, low = split(jnp.concatenate(lines, axis=0))
+        both = dot(jnp.concatenate([high, low], axis=0), x_high[scale])
+        product = both[: ROWS // 2] + both[ROWS // 2 :] + dot(high, x_low[scale])
+        for r in range(2):
+            for half in range(2):
+                fields[places[r][half], :] = product[
+                    ROWS // 4 * r : ROWS // 4 * (r + 1), 128 * half : 128 * (half + 1)
+                ]
+        return carry
+
+    lax.fori_loop(0, LEVELS, level, 0, unroll=4)
+
+
+def adjoint_kernel(
+    core_ref,
+    scale_ref,
+    dir_ref,
+    perturb_ref,
+    matrix_ref,
+    smooth_x_ref,
+    early_ref,
+    out_ref,
+    lines,
+    controls,
+    result,
+    x_high,
+    x_low,
+    in_sem,
+    out_sem,
+):
+    del early_ref
     pieces = []
     for c in range(8):
         part = pl.ds(8 * c, 8)
@@ -92,56 +141,74 @@
     for c in range(8):
         pieces[c].wait()
         lax.fori_loop(8 * c, 8 * c + 8, level, 0, unroll=2)
-    vertical_product(
-        matrix_ref[...].T, controls, result, lambda step: send_rows(result, out_ref, out_sem, step).start()
-    )
-    wait_rows(result, out_ref, out_sem)
+    vertical_product(matrix_ref[...].T, controls, result)
+
+    @pl.when(core_ref[0] == 1)
+    def _():
+        smooth_along_x(scale_ref, smooth_x_ref, result, x_high, x_low)
+
+    for step in range(ROWS // WIDE_GROUP):
+        send_rows(result, out_ref, out_sem, step, WIDE_GROUP).start()
+    wait_rows(result, out_ref, out_sem, WIDE_GROUP)
+
+
+def chosen_covariance(scale, matrix):
+    power = matrix
+    chosen = matrix
+    for step in range(2, 5):
+        power = jnp.dot(matrix, power, precision=lax.Precision.HIGHEST, preferred_element_type=F32)
+        chosen = jnp.where(scale == step, power, chosen)
+    return split(outer(chosen))
+
+
+def prepare_y_kernel(scale_ref, smooth_y_ref, y_ref):
+    high, low = chosen_covariance(scale_ref[0], smooth_y_ref[...])
+    y_ref[...] = jnp.concatenate([high, high, low], axis=1)
 
 
 def prepare_kernel(scale_ref, smooth_y_ref, smooth_x_ref, y_ref, xh_ref, xl_ref):
-    scale = scale_ref[0]
-
-    def covariance(matrix):
-        power = matrix
-        chosen = matrix
-        for step in range(2, 5):
-            power = jnp.dot(matrix, power, precision=lax.Precision.HIGHEST, preferred_element_type=F32)
-            chosen = jnp.where(scale == step, power, chosen)
-        return lax.dot_general(
-            chosen, chosen, (((1,), (1,)), ((), ())), precision=lax.Precision.HIGHEST, preferred_element_type=F32
-        )
-
-    high, low = split(covariance(smooth_y_ref[...]))
-    y_ref[...] = jnp.concatenate([high, high, low], axis=1)
-    high, low = split(covariance(smooth_x_ref[...]))
+    prepare_y_kernel(scale_ref, smooth_y_ref, y_ref)
+    high, low = chosen_covariance(scale_ref[0], smooth_x_ref[...])
     xh_ref[...] = high
     xl_ref[...] = low
 
 
-def smooth_kernel(in_ref, y_ref, xh_ref, xl_ref, spent_ref, out_ref, source, result, out_sem):
+def smooth_kernel(core_ref, in_ref, y_ref, xh_ref, xl_ref, spent_ref, out_ref, source, result, out_sem):
     del spent_ref
-    xh, xl = xh_ref[...], xl_ref[...]
-    y_both, y_low = y_ref[:, :256], y_ref[:, 256:]
     spread(in_ref, source)
-    for step in range(ROWS // 4 // MEMBERS_AT_ONCE):
-        first = step * MEMBERS_AT_ONCE * 4
-        halves = []
-        for k in range(MEMBERS_AT_ONCE):
-            for r in range(2):
-                parts = [source[every_level(first + 4 * k + 2 * half + r), :] for half in range(2)]
-                halves.append(jnp.concatenate(parts, axis=1))
-        high, low = split(jnp.concatenate(halves, axis=0))
-        along_x = dot(high, xh) + dot(low, xh) + dot(high, xl)
-        for k in range(MEMBERS_AT_ONCE):
-            high, low = split(along_x[128 * k : 128 * (k + 1)])
-            smoothed = dot(y_both, jnp.concatenate([high, low], axis=0)) + dot(y_low, high)
-            for r in range(2):
-                for half in range(2):
-                    result[every_level(first + 4 * k + 2 * half + r), :] = smoothed[
-                        64 * r : 64 * (r + 1), 128 * half : 128 * (half + 1)
-                    ]
-        send_rows(result, out_ref, out_sem, step, 4 * MEMBERS_AT_ONCE).start()
-    wait_rows(result, out_ref, out_sem, 4 * MEMBERS_AT_ONCE)
+
+    def run(with_x):
+        y_both, y_low = y_ref[:, :256], y_ref[:, 256:]
+        for step in range(ROWS // WIDE_GROUP):
+            first = step * WIDE_GROUP
+            halves = []
+            for k in range(MEMBERS_AT_ONCE):
+                for r in range(2):
+                    parts = [source[every_level(first + 4 * k + 2 * half + r), :] for half in range(2)]
+                    halves.append(jnp.concatenate(parts, axis=1))
+            fields = jnp.concatenate(halves, axis=0)
+            if with_x:
+                high, low = split(fields)
+                fields = dot(high, xh_ref[...]) + dot(low, xh_ref[...]) + dot(high, xl_ref[...])
+            for k in range(MEMBERS_AT_ONCE):
+                high, low = split(fields[128 * k : 128 * (k + 1)])
+                smoothed = dot(y_both, jnp.concatenate([high, low], axis=0)) + dot(y_low, high)
+                for r in range(2):
+                    for half in range(2):
+                        result[every_level(first + 4 * k + 2 * half + r), :] = smoothed[
+                            64 * r : 64 * (r + 1), 128 * half : 128 * (half + 1)
+                        ]
+            send_rows(result, out_ref, out_sem, step, WIDE_GROUP).start()
+
+    @pl.when(core_ref[0] == 0)
+    def _():
+        run(True)
+
+    @pl.when(core_ref[0] == 1)
+    def _():
+        run(False)
+
+    wait_rows(result, out_ref, out_sem, WIDE_GROUP)
 
 
 def fetch_levels(parity, perturb_ref, lines, sem):
@@ -196,6 +263,7 @@
 SPREAD = jax.ShapeDtypeStruct((LEVELS * PITCH, 128), F32)
 SPREAD_SCRATCH = pltpu.VMEM(SPREAD.shape, F32)
 HALF_SCRATCH = pltpu.VMEM((4, VARS, 8, ROWS, 128), BF16)
+X_SCRATCH = pltpu.VMEM((4, 256, 256), BF16)
 DMA = pltpu.SemaphoreType.DMA
 
 
@@ -216,32 +284,31 @@
 adjoint_call = call(
     adjoint_kernel,
     "adjoint",
-    [VMEM, HBM, VMEM],
+    [SMEM, SMEM, VMEM, HBM, VMEM, VMEM, HBM],
     [(HBM, FIELDS)],
     300_000_000,
-    [pltpu.VMEM((VARS, LEVELS, ROWS, 128), BF16), SPREAD_SCRATCH, SPREAD_SCRATCH, DMA((8,)), DMA((8,))],
+    [pltpu.VMEM((VARS, LEVELS, ROWS, 128), BF16), SPREAD_SCRATCH, SPREAD_SCRATCH, X_SCRATCH, X_SCRATCH, DMA((8,)), DMA((4,))],
     vmem=60,
 )
+COV_Y = jax.ShapeDtypeStruct((128, 384), BF16)
+COV_X = jax.ShapeDtypeStruct((256, 256), BF16)
+prepare_y_call = call(prepare_y_kernel, "prepare_y", [SMEM, VMEM], [(VMEM, COV_Y)], 300_000_000)
 prepare_call = call(
     prepare_kernel,
     "prepare",
     [SMEM, VMEM, VMEM],
-    [
-        (VMEM, jax.ShapeDtypeStruct((128, 384), BF16)),
-        (VMEM, jax.ShapeDtypeStruct((256, 256), BF16)),
-        (VMEM, jax.ShapeDtypeStruct((256, 256), BF16)),
-    ],
+    [(VMEM, COV_Y), (VMEM, COV_X), (VMEM, COV_X)],
     1_000_000_000,
 )
 smooth_call = call(
     smooth_kernel,
     "smooth",
-    [VMEM] * 4 + [HBM],
+    [SMEM] + [VMEM] * 4 + [HBM],
     [(HBM, FIELDS)],
     1_200_000_000,
     [SPREAD_SCRATCH, SPREAD_SCRATCH, DMA((4,))],
     vmem=48,
-    aliases={4: 0},
+    aliases={5: 0},
 )
 give_call = call(
     give_kernel,
@@ -285,13 +352,21 @@
     core = lax.rem(lax.axis_index("mem"), 2)[None]
     lines = to_lines(perturb).reshape(VARS, LEVELS, ROWS, 128)
     full_dir = lax.all_gather(to_lines(search_dir), "mem", axis=1, tiled=True)
-    adjoint = adjoint_call(full_dir, lines, vertical)
-
-    scale = lax.dynamic_slice_in_dim(level_scale, lax.axis_index("tile"), 1)
-    ordered_y = smooth_y.reshape(64, 2, 64, 2).transpose(1, 0, 3, 2).reshape(128, 128)
-    cov_y, cov_xh, cov_xl = prepare_call(scale, ordered_y, smooth_x)
-
-    smoothed = smooth_call(flat(exchange(adjoint)), cov_y, cov_xh, cov_xl, adjoint)
+
+    def scale_and_y():
+        scale = lax.dynamic_slice_in_dim(level_scale, lax.axis_index("tile"), 1)
+        return scale, smooth_y.reshape(64, 2, 64, 2).transpose(1, 0, 3, 2).reshape(128, 128)
+
+    second = core[0] == 1
+    early = lax.cond(second, lambda: prepare_y_call(*scale_and_y()), lambda: jnp.zeros(COV_Y.shape, BF16))
+    adjoint = adjoint_call(core, level_scale, full_dir, lines, vertical, smooth_x, early)
+    cov_y, cov_xh, cov_xl = lax.cond(
+        second,
+        lambda: [early, jnp.zeros(COV_X.shape, BF16), jnp.zeros(COV_X.shape, BF16)],
+        lambda: list(prepare_call(*scale_and_y(), smooth_x)),
+    )
+
+    smoothed = smooth_call(core, flat(exchange(adjoint)), cov_y, cov_xh, cov_xl, adjoint)
     forward, give = give_call(core, flat(exchange(smoothed)), lines, vertical)
     keep = keep_call(core, forward, lines)
     both = keep + lax.ppermute(give, "mem", [(m, m ^ 1) for m in range(8)])

time: 268 us -> 263 us (0.981)
  blocking collectives: 31.4 us -> 130 us
  waiting for transfers between devices: 179 us -> 82.9 us
  starting transfers between devices: 30.5 us -> 15.7 us
  Pallas kernels: 17.1 us -> 22.7 us
    all_to_all x0 -> x1, blocking collectives: none -> 98.5 us  [exchange(): lax.all_to_all(fields, 'tile', split_axis=0, concat_axis=0, tiled=True)]
    all_to_all x2 -> x1, waiting for transfers between devices: 179 us -> 82.9 us  [exchange(): lax.all_to_all(fields, 'tile', split_axis=0, concat_axis=0, tiled=True)]
    all_to_all x2 -> x1, starting transfers between devices: 22.1 us -> 13.8 us  [exchange(): lax.all_to_all(fields, 'tile', split_axis=0, concat_axis=0, tiled=True)]
    ppermute x1, starting transfers between devices: 8.35 us -> 1.92 us  [per_device(): both = keep + lax.ppermute(give, 'mem', [(m, m ^ 1) for m in range(8)])]
    pallas_call x3, Pallas kernels: 12.7 us -> 18.3 us  [the longest x1 13.1 us: per_device(): adjoint_call(core, level_scale, full_dir, lines, vertical, smooth_x, early)]
  transfers between devices with their start and end apart: 3 -> 2, of which waited for: 2 -> 1; matrix products, arithmetic and copies ran while one was open for 3% -> 0% of each run, Pallas kernels for 2% -> 1%
where the time goes in v4:
time: 263 us; the launch traced here: 262 us
  blocking collectives  130 us (49%)
  waiting for transfers between devices  82.9 us (32%)
  Pallas kernels  22.7 us (9%)
  starting transfers between devices  15.7 us (6%)
  local copies, waits for them, and re-layouts  10.7 us (4%)
    all_to_all x1, blocking collectives, exchange(): lax.all_to_all(fields, 'tile', split_axis=0, concat_axis=0, tiled=True)  98.5 us
    all_to_all x1, waiting for transfers between devices, exchange(): lax.all_to_all(fields, 'tile', split_axis=0, concat_axis=0, tiled=True)  82.9 us
    all_gather x1, blocking collectives, per_device(): full_dir = lax.all_gather(to_lines(search_dir), 'mem', axis=1, tiled=True)  21.3 us
    all_to_all x1, starting transfers between devices, exchange(): lax.all_to_all(fields, 'tile', split_axis=0, concat_axis=0, tiled=True)  13.8 us
    pallas_call x1, Pallas kernels, per_device(): adjoint_call(core, level_scale, full_dir, lines, vertical, smooth_x, early)  13.1 us
    all_to_all x1, blocking collectives, per_device(): lax.all_to_all(both, 'mem', split_axis=0, concat_axis=0, tiled=True, axis...  9.88 us
    reshape x2, local copies, waits for them, and re-layouts, scale_and_y(): smooth_y.reshape(64, 2, 64, 2).transpose(1, 0, 3, 2).reshape(128, 128)  6.38 us
  transfers between devices with their start and end apart: 2, of which 1 were waited for; matrix products, arithmetic and copies ran while one was open for 0% of the time, Pallas kernels for 1%

profile of v4, /device:TPU:1, one launch (start us, length us, event | category | flops | bytes accessed | tf_op | source)
XLA Modules:
  0.0 262.1 jit_solution(15880397080887927361)
XLA Ops:
  0.0 21.3 %all_gather.3.dir_ref = f32[5,64,4,128]{3,2,1,0:T(4,128)} all-gather(f32[5,8,4,128]{3,2,1,0:T(4,128)} %bitcast.26), channel_id=1, replica_groups=mesh['tile'=64,'mem'=8] {'mem'}, dimensions={1}, use_global_device_ids=true | all-gather | bytes 737280 | tf_op jit(solution)/shard_map/all_gather | solution.py:354
  21.3 12.3 %conditional.2 = (bf16[128,384]{1,0:T(8,128)(2,1)S(1)}) conditional(s32[]{:T(128)} %convert_element_type.4, () %tuple.18, (s32[64]{0:T(128)}, f32[128,128]{1,0:T(8,128)}) %tuple.19), branch_computations={%region_0.0_spmd, %region_1.0_spmd} | conditional | flops 300000000 | bytes 4393302 | solution.py:361
  21.3 1.3 dynamic_slice.4.scale_ref
  22.6 6.3 %reshape.22 = f32[64,2,64,2]{3,2,1,0:T(8,128)} reshape(f32[128,128]{1,0:T(8,128)} %get-tuple-element.20) | data formatting | bytes 131072 | tf_op jit(solution)/shard_map/cond/branch_1_fun/reshape | solution.py:358
  28.8 3.0 %copy.13 = f32[2,64,2,64]{3,2,1,0:T(2,128)S(1)} copy(f32[2,64,2,64]{2,3,0,1:T(8,128)} %bitcast.24) | data formatting | bytes 131072 | tf_op jit(solution)/shard_map/cond/branch_1_fun/transpose | solution.py:358
  31.8 0.1 reshape.23.smooth_y_ref
  32.0 1.6 prepare_y.1
  33.6 13.1 %adjoint.1.spent_ref = f32[64,64,128]{2,1,0:T(8,128)} custom-call(s32[1]{0:T(128)} %bitcast.2.core_ref, s32[64]{0:T(128)} %scale_ref.1, f32[5,64,4,128]{3,2,1,0:T(4,128)} %all_gather.3.dir_ref, bf16[5,64,64,128]{3,2,1,0:T(8,128)(2,1)} %bitcast.21, f32[64,64]{1,0:T(8,128)} %matrix_ref.3, f32[256,256]{1,0:T(8,128)S(1)} %copy-done.3, ...), custom_call_target="tpu_custom_call" | custom-call | flops 300000000 | bytes 4000000 | tf_op jit(solution)/shard_map/adjoint/pallas_call | solution.py:362
  46.7 0.0 copy-start.2
  46.7 0.0 copy-start.4
  46.7 13.8 %all-to-all-start = ((f32[64,64,128]{2,1,0:T(8,128)}), f32[64,64,128]{2,1,0:T(8,128)}, u32[]{:S(2)}, u32[]{:S(2)}) async-start(f32[64,64,128]{2,1,0:T(8,128)} %adjoint.1.spent_ref), calls=%async_computation | async-start | bytes 4194304 | tf_op jit(solution)/shard_map/all_to_all | solution.py:344
  60.6 0.0 copy-done.2
  60.6 0.1 conditional.3
  60.6 82.9 %all-to-all-done = f32[64,64,128]{2,1,0:T(8,128)} async-done(((f32[64,64,128]{2,1,0:T(8,128)}), f32[64,64,128]{2,1,0:T(8,128)}, u32[]{:S(2)}, u32[]{:S(2)}) %all-to-all-start) | async-done | bytes 2097184 | tf_op jit(solution)/shard_map/all_to_all | solution.py:344
  143.5 3.6 %smooth.1 = f32[64,64,128]{2,1,0:T(8,128)S(1)} custom-call(s32[1]{0:T(128)} %bitcast.2.core_ref, f32[4096,128]{1,0:T(8,128)} %bitcast.9.in_ref, bf16[128,384]{1,0:T(8,128)(2,1)S(1)} %get-tuple-element.29.y_ref, bf16[256,256]{1,0:T(8,128)(2,1)S(1)} %get-tuple-element.30.xh_ref, ...), custom_call_target="tpu_custom_call", output_to_operand_aliasing={{}: (5, {})} | custom-call | flops 1200000000 | bytes 4000000 | tf_op jit(solution)/shard_map/smooth/pallas_call | solution.py:369
  147.1 0.0 copy-start.1
  147.2 98.5 %all_to_all.15 = f32[64,64,128]{2,1,0:T(8,128)S(1)} all-to-all(f32[64,64,128]{2,1,0:T(8,128)S(1)} %smooth.1), channel_id=1, replica_groups=mesh['tile'=64,'mem'=8] {'tile'}, dimensions={0} | all-to-all | bytes 4194304 | tf_op jit(solution)/shard_map/all_to_all | solution.py:344
  245.7 1.9 give.1
  247.6 1.9 collective-permute-start
  249.5 1.9 keep.1
  251.4 0.0 collective-permute-done
  251.4 0.1 add.9
  251.5 9.9 %all_to_all.16.in_ref = f32[4,5,8,4,128]{4,3,2,1,0:T(4,128)S(1)} all-to-all(f32[4,5,8,4,128]{4,3,2,1,0:T(4,128)S(1)} %add.9), channel_id=1, replica_groups={{0,2,4,6},{1,3,5,7},{8,10,12,14},{9,11,13,15},{16,18,20,22},{17,19,21,2..., dimensions={0} | all-to-all | bytes 655360 | tf_op jit(solution)/shard_map/all_to_all | solution.py:373
  261.4 0.7 finish.1
  (8 shorter events, 0.0 us)
Async XLA Ops:
  21.3 12.3 %copy-start.3 = (f32[256,256]{1,0:T(8,128)S(1)}, f32[256,256]{1,0:T(8,128)}, u32[]{:S(2)}) copy-start(f32[256,256]{1,0:T(8,128)} %smooth_x_ref.1) | copy-start | bytes 786436
  46.7 13.9 %copy-start.2 = (f32[128,128]{1,0:T(8,128)S(1)}, f32[128,128]{1,0:T(8,128)}, u32[]{:S(2)}) copy-start(f32[128,128]{1,0:T(8,128)} %param.12) | copy-start | bytes 196612
  46.7 13.9 %copy-start.4 = (s32[64]{0:T(128)S(1)}, s32[64]{0:T(128)}, u32[]{:S(2)}) copy-start(s32[64]{0:T(128)} %scale_ref.1) | copy-start | bytes 772
  46.7 96.8 %all-to-all-start = ((f32[64,64,128]{2,1,0:T(8,128)}), f32[64,64,128]{2,1,0:T(8,128)}, u32[]{:S(2)}, u32[]{:S(2)}) async-start(f32[64,64,128]{2,1,0:T(8,128)} %adjoint.1.spent_ref), calls=%async_computation | async-start | bytes 4194304 | tf_op jit(solution)/shard_map/all_to_all | solution.py:344
  60.6 83.0 %copy-start = (f32[64,64,128]{2,1,0:T(8,128)S(1)}, f32[64,64,128]{2,1,0:T(8,128)}, u32[]{:S(2)}) copy-start(f32[64,64,128]{2,1,0:T(8,128)} %adjoint.1.spent_ref) | copy-start | bytes 6291460
  147.1 98.6 %copy-start.1 = (f32[64,64]{1,0:T(8,128)S(1)}, f32[64,64]{1,0:T(8,128)}, u32[]{:S(2)}) copy-start(f32[64,64]{1,0:T(8,128)} %matrix_ref.3) | copy-start | bytes 49156
  247.6 3.8 %collective-permute-start = (f32[4,5,8,4,128]{4,3,2,1,0:T(4,128)S(1)}, f32[4,5,8,4,128]{4,3,2,1,0:T(4,128)S(1)}, u32[]{:S(2)}, u32[]{:S(2)}) collective-permute-start(f32[4,5,8,4,128]{4,3,2,1,0:T(4,128)S(1)} %get-tuple-element.33), channel_id=1, source_target_pairs={{0,1},{1,0},{2,3},{3,2},{4,5},{5,4},{6,7},{7,6},{8,9},{9,8},{10,11... | collective-permute-start | bytes 983048 | tf_op jit(solution)/shard_map/ppermute | solution.py:372

commit v5 on v4

--- a/solution.py
+++ b/solution.py
@@ -77,23 +77,24 @@
         send_rows(result, out_ref, sem, step, count).wait()
 
 
-def smooth_along_x(scale_ref, smooth_x_ref, fields, x_high, x_low):
+def smooth_along_x(scale_ref, smooth_x_ref, fields, covariances):
     matrix = smooth_x_ref[...]
     power = matrix
     for step in range(4):
         if step:
             power = jnp.dot(matrix, power, precision=lax.Precision.HIGHEST, preferred_element_type=F32)
-        high, low = split(outer(power))
-        x_high[step] = high
-        x_low[step] = low
+        covariances[step] = outer(power)
 
     def level(q, carry):
         scale = scale_ref[q] - 1
         places = [[pl.ds(q * PITCH + 2 * half + r, ROWS // 4, stride=4) for half in range(2)] for r in range(2)]
         lines = [jnp.concatenate([fields[place, :] for place in pair], axis=1) for pair in places]
-        high, low = split(jnp.concatenate(lines, axis=0))
-        both = dot(jnp.concatenate([high, low], axis=0), x_high[scale])
-        product = both[: ROWS // 2] + both[ROWS // 2 :] + dot(high, x_low[scale])
+        product = jnp.dot(
+            jnp.concatenate(lines, axis=0),
+            covariances[scale],
+            precision=lax.Precision.HIGHEST,
+            preferred_element_type=F32,
+        )
         for r in range(2):
             for half in range(2):
                 fields[places[r][half], :] = product[
@@ -116,8 +117,7 @@
     lines,
     controls,
     result,
-    x_high,
-    x_low,
+    covariances,
     in_sem,
     out_sem,
 ):
@@ -145,7 +145,7 @@
 
     @pl.when(core_ref[0] == 1)
     def _():
-        smooth_along_x(scale_ref, smooth_x_ref, result, x_high, x_low)
+        smooth_along_x(scale_ref, smooth_x_ref, result, covariances)
 
     for step in range(ROWS // WIDE_GROUP):
         send_rows(result, out_ref, out_sem, step, WIDE_GROUP).start()
@@ -263,7 +263,7 @@
 SPREAD = jax.ShapeDtypeStruct((LEVELS * PITCH, 128), F32)
 SPREAD_SCRATCH = pltpu.VMEM(SPREAD.shape, F32)
 HALF_SCRATCH = pltpu.VMEM((4, VARS, 8, ROWS, 128), BF16)
-X_SCRATCH = pltpu.VMEM((4, 256, 256), BF16)
+X_SCRATCH = pltpu.VMEM((4, 256, 256), F32)
 DMA = pltpu.SemaphoreType.DMA
 
 
@@ -287,7 +287,7 @@
     [SMEM, SMEM, VMEM, HBM, VMEM, VMEM, HBM],
     [(HBM, FIELDS)],
     300_000_000,
-    [pltpu.VMEM((VARS, LEVELS, ROWS, 128), BF16), SPREAD_SCRATCH, SPREAD_SCRATCH, X_SCRATCH, X_SCRATCH, DMA((8,)), DMA((4,))],
+    [pltpu.VMEM((VARS, LEVELS, ROWS, 128), BF16), SPREAD_SCRATCH, SPREAD_SCRATCH, X_SCRATCH, DMA((8,)), DMA((4,))],
     vmem=60,
 )
 COV_Y = jax.ShapeDtypeStruct((128, 384), BF16)

time: 263 us -> 258 us (0.981)
  waiting for transfers between devices: 82.9 us -> 77 us
  Pallas kernels: 22.7 us -> 28.6 us
  blocking collectives: 130 us -> 125 us
    all_to_all x1, waiting for transfers between devices: 82.9 us -> 77 us  [exchange(): lax.all_to_all(fields, 'tile', split_axis=0, concat_axis=0, tiled=True)]
    pallas_call x1, Pallas kernels: 13.1 us -> 19 us  [per_device(): adjoint_call(core, level_scale, full_dir, lines, vertical, smooth_x, early)]
    all_to_all x1, blocking collectives: 98.5 us -> 93.5 us  [exchange(): lax.all_to_all(fields, 'tile', split_axis=0, concat_axis=0, tiled=True)]
where the time goes in v5:
time: 258 us; the launch traced here: 257 us
  blocking collectives  125 us (48%)
  waiting for transfers between devices  77 us (30%)
  Pallas kernels  28.6 us (11%)
  starting transfers between devices  15.7 us (6%)
  local copies, waits for them, and re-layouts  10.7 us (4%)
    all_to_all x1, blocking collectives, exchange(): lax.all_to_all(fields, 'tile', split_axis=0, concat_axis=0, tiled=True)  93.5 us
    all_to_all x1, waiting for transfers between devices, exchange(): lax.all_to_all(fields, 'tile', split_axis=0, concat_axis=0, tiled=True)  77 us
    all_gather x1, blocking collectives, per_device(): full_dir = lax.all_gather(to_lines(search_dir), 'mem', axis=1, tiled=True)  21.3 us
    pallas_call x1, Pallas kernels, per_device(): adjoint_call(core, level_scale, full_dir, lines, vertical, smooth_x, early)  19 us
    all_to_all x1, starting transfers between devices, exchange(): lax.all_to_all(fields, 'tile', split_axis=0, concat_axis=0, tiled=True)  13.8 us
    all_to_all x1, blocking collectives, per_device(): lax.all_to_all(both, 'mem', split_axis=0, concat_axis=0, tiled=True, axis...  9.8 us
    reshape x2, local copies, waits for them, and re-layouts, scale_and_y(): smooth_y.reshape(64, 2, 64, 2).transpose(1, 0, 3, 2).reshape(128, 128)  6.38 us
  transfers between devices with their start and end apart: 2, of which 1 were waited for; matrix products, arithmetic and copies ran while one was open for 0% of the time, Pallas kernels for 1%

profile of v5, /device:TPU:1, one launch (start us, length us, event | category | flops | bytes accessed | tf_op | source)
XLA Modules:
  0.0 256.9 jit_solution(12492268685829719938)
XLA Ops:
  0.0 21.3 %all_gather.3.dir_ref = f32[5,64,4,128]{3,2,1,0:T(4,128)} all-gather(f32[5,8,4,128]{3,2,1,0:T(4,128)} %bitcast.26), channel_id=1, replica_groups=mesh['tile'=64,'mem'=8] {'mem'}, dimensions={1}, use_global_device_ids=true | all-gather | bytes 737280 | tf_op jit(solution)/shard_map/all_gather | solution.py:354
  21.3 12.3 %conditional.2 = (bf16[128,384]{1,0:T(8,128)(2,1)S(1)}) conditional(s32[]{:T(128)} %convert_element_type.4, () %tuple.18, (s32[64]{0:T(128)}, f32[128,128]{1,0:T(8,128)}) %tuple.19), branch_computations={%region_0.0_spmd, %region_1.0_spmd} | conditional | flops 300000000 | bytes 4393302 | solution.py:361
  21.3 1.3 dynamic_slice.4.scale_ref
  22.6 6.3 %reshape.22 = f32[64,2,64,2]{3,2,1,0:T(8,128)} reshape(f32[128,128]{1,0:T(8,128)} %get-tuple-element.20) | data formatting | bytes 131072 | tf_op jit(solution)/shard_map/cond/branch_1_fun/reshape | solution.py:358
  28.8 3.0 %copy.13 = f32[2,64,2,64]{3,2,1,0:T(2,128)S(1)} copy(f32[2,64,2,64]{2,3,0,1:T(8,128)} %bitcast.24) | data formatting | bytes 131072 | tf_op jit(solution)/shard_map/cond/branch_1_fun/transpose | solution.py:358
  31.8 0.1 reshape.23.smooth_y_ref
  32.0 1.6 prepare_y.1
  33.6 19.0 %adjoint.1.spent_ref = f32[64,64,128]{2,1,0:T(8,128)} custom-call(s32[1]{0:T(128)} %bitcast.2.core_ref, s32[64]{0:T(128)} %scale_ref.1, f32[5,64,4,128]{3,2,1,0:T(4,128)} %all_gather.3.dir_ref, bf16[5,64,64,128]{3,2,1,0:T(8,128)(2,1)} %bitcast.21, f32[64,64]{1,0:T(8,128)} %matrix_ref.3, f32[256,256]{1,0:T(8,128)S(1)} %copy-done.3, ...), custom_call_target="tpu_custom_call" | custom-call | flops 300000000 | bytes 4000000 | tf_op jit(solution)/shard_map/adjoint/pallas_call | solution.py:362
  52.5 0.0 copy-start.2
  52.6 0.0 copy-start.4
  52.6 13.8 %all-to-all-start = ((f32[64,64,128]{2,1,0:T(8,128)}), f32[64,64,128]{2,1,0:T(8,128)}, u32[]{:S(2)}, u32[]{:S(2)}) async-start(f32[64,64,128]{2,1,0:T(8,128)} %adjoint.1.spent_ref), calls=%async_computation | async-start | bytes 4194304 | tf_op jit(solution)/shard_map/all_to_all | solution.py:344
  66.4 0.1 conditional.3
  66.5 77.0 %all-to-all-done = f32[64,64,128]{2,1,0:T(8,128)} async-done(((f32[64,64,128]{2,1,0:T(8,128)}), f32[64,64,128]{2,1,0:T(8,128)}, u32[]{:S(2)}, u32[]{:S(2)}) %all-to-all-start) | async-done | bytes 2097184 | tf_op jit(solution)/shard_map/all_to_all | solution.py:344
  143.5 0.0 copy-done
  143.5 3.6 %smooth.1 = f32[64,64,128]{2,1,0:T(8,128)S(1)} custom-call(s32[1]{0:T(128)} %bitcast.2.core_ref, f32[4096,128]{1,0:T(8,128)} %bitcast.9.in_ref, bf16[128,384]{1,0:T(8,128)(2,1)S(1)} %get-tuple-element.29.y_ref, bf16[256,256]{1,0:T(8,128)(2,1)S(1)} %get-tuple-element.30.xh_ref, ...), custom_call_target="tpu_custom_call", output_to_operand_aliasing={{}: (5, {})} | custom-call | flops 1200000000 | bytes 4000000 | tf_op jit(solution)/shard_map/smooth/pallas_call | solution.py:369
  147.1 0.0 copy-start.1
  147.2 93.5 %all_to_all.15 = f32[64,64,128]{2,1,0:T(8,128)S(1)} all-to-all(f32[64,64,128]{2,1,0:T(8,128)S(1)} %smooth.1), channel_id=1, replica_groups=mesh['tile'=64,'mem'=8] {'tile'}, dimensions={0} | all-to-all | bytes 4194304 | tf_op jit(solution)/shard_map/all_to_all | solution.py:344
  240.6 1.9 give.1
  242.5 1.9 collective-permute-start
  244.5 1.9 keep.1
  246.3 0.0 collective-permute-done
  246.4 0.1 add.9
  246.5 9.8 %all_to_all.16.in_ref = f32[4,5,8,4,128]{4,3,2,1,0:T(4,128)S(1)} all-to-all(f32[4,5,8,4,128]{4,3,2,1,0:T(4,128)S(1)} %add.9), channel_id=1, replica_groups={{0,2,4,6},{1,3,5,7},{8,10,12,14},{9,11,13,15},{16,18,20,22},{17,19,21,2..., dimensions={0} | all-to-all | bytes 655360 | tf_op jit(solution)/shard_map/all_to_all | solution.py:373
  256.3 0.7 finish.1
  (8 shorter events, 0.0 us)
Async XLA Ops:
  21.3 12.3 %copy-start.3 = (f32[256,256]{1,0:T(8,128)S(1)}, f32[256,256]{1,0:T(8,128)}, u32[]{:S(2)}) copy-start(f32[256,256]{1,0:T(8,128)} %smooth_x_ref.1) | copy-start | bytes 786436
  52.5 13.9 %copy-start.2 = (f32[128,128]{1,0:T(8,128)S(1)}, f32[128,128]{1,0:T(8,128)}, u32[]{:S(2)}) copy-start(f32[128,128]{1,0:T(8,128)} %param.12) | copy-start | bytes 196612
  52.6 13.9 %copy-start.4 = (s32[64]{0:T(128)S(1)}, s32[64]{0:T(128)}, u32[]{:S(2)}) copy-start(s32[64]{0:T(128)} %scale_ref.1) | copy-start | bytes 772
  52.6 91.0 %all-to-all-start = ((f32[64,64,128]{2,1,0:T(8,128)}), f32[64,64,128]{2,1,0:T(8,128)}, u32[]{:S(2)}, u32[]{:S(2)}) async-start(f32[64,64,128]{2,1,0:T(8,128)} %adjoint.1.spent_ref), calls=%async_computation | async-start | bytes 4194304 | tf_op jit(solution)/shard_map/all_to_all | solution.py:344
  66.4 77.1 %copy-start = (f32[64,64,128]{2,1,0:T(8,128)S(1)}, f32[64,64,128]{2,1,0:T(8,128)}, u32[]{:S(2)}) copy-start(f32[64,64,128]{2,1,0:T(8,128)} %adjoint.1.spent_ref) | copy-start | bytes 6291460
  147.1 93.5 %copy-start.1 = (f32[64,64]{1,0:T(8,128)S(1)}, f32[64,64]{1,0:T(8,128)}, u32[]{:S(2)}) copy-start(f32[64,64]{1,0:T(8,128)} %matrix_ref.3) | copy-start | bytes 49156
  242.5 3.8 %collective-permute-start = (f32[4,5,8,4,128]{4,3,2,1,0:T(4,128)S(1)}, f32[4,5,8,4,128]{4,3,2,1,0:T(4,128)S(1)}, u32[]{:S(2)}, u32[]{:S(2)}) collective-permute-start(f32[4,5,8,4,128]{4,3,2,1,0:T(4,128)S(1)} %get-tuple-element.33), channel_id=1, source_target_pairs={{0,1},{1,0},{2,3},{3,2},{4,5},{5,4},{6,7},{7,6},{8,9},{9,8},{10,11... | collective-permute-start | bytes 983048 | tf_op jit(solution)/shard_map/ppermute | solution.py:372

commit v6 on v5

--- a/solution.py
+++ b/solution.py
@@ -141,10 +141,27 @@
     for c in range(8):
         pieces[c].wait()
         lax.fori_loop(8 * c, 8 * c + 8, level, 0, unroll=2)
-    vertical_product(matrix_ref[...].T, controls, result)
+    matrix = matrix_ref[...].T
+
+    @pl.when(core_ref[0] == 0)
+    def _():
+        vertical_product(matrix, controls, result)
 
     @pl.when(core_ref[0] == 1)
     def _():
+        def pair(step, carry):
+            parts = [controls[every_level(2 * step + i), :] for i in range(2)]
+            product = jnp.dot(
+                matrix,
+                jnp.concatenate(parts, axis=1),
+                precision=lax.Precision.HIGHEST,
+                preferred_element_type=F32,
+            )
+            for i in range(2):
+                result[every_level(2 * step + i), :] = product[:, 128 * i : 128 * (i + 1)]
+            return carry
+
+        lax.fori_loop(0, ROWS // 2, pair, 0, unroll=4)
         smooth_along_x(scale_ref, smooth_x_ref, result, covariances)
 
     for step in range(ROWS // WIDE_GROUP):

time: 258 us -> 257 us (level)
  no operation moved by 1% of the time
where the time goes in v6:
time: 257 us; the launch traced here: 255 us
  blocking collectives  123 us (48%)
  waiting for transfers between devices  75.1 us (29%)
  Pallas kernels  30.6 us (12%)
  starting transfers between devices  15.7 us (6%)
  local copies, waits for them, and re-layouts  10.7 us (4%)
    all_to_all x1, blocking collectives, exchange(): lax.all_to_all(fields, 'tile', split_axis=0, concat_axis=0, tiled=True)  91.5 us
    all_to_all x1, waiting for transfers between devices, exchange(): lax.all_to_all(fields, 'tile', split_axis=0, concat_axis=0, tiled=True)  75.1 us
    all_gather x1, blocking collectives, per_device(): full_dir = lax.all_gather(to_lines(search_dir), 'mem', axis=1, tiled=True)  21.3 us
    pallas_call x1, Pallas kernels, per_device(): adjoint_call(core, level_scale, full_dir, lines, vertical, smooth_x, early)  21 us
    all_to_all x1, starting transfers between devices, exchange(): lax.all_to_all(fields, 'tile', split_axis=0, concat_axis=0, tiled=True)  13.8 us
    all_to_all x1, blocking collectives, per_device(): lax.all_to_all(both, 'mem', split_axis=0, concat_axis=0, tiled=True, axis...  9.85 us
    reshape x2, local copies, waits for them, and re-layouts, scale_and_y(): smooth_y.reshape(64, 2, 64, 2).transpose(1, 0, 3, 2).reshape(128, 128)  6.38 us
  transfers between devices with their start and end apart: 2, of which 1 were waited for; matrix products, arithmetic and copies ran while one was open for 0% of the time, Pallas kernels for 1%

profile of v6, /device:TPU:1, one launch (start us, length us, event | category | flops | bytes accessed | tf_op | source)
XLA Modules:
  0.0 255.1 jit_solution(259263315101733033)
XLA Ops:
  0.0 21.3 %all_gather.3.dir_ref = f32[5,64,4,128]{3,2,1,0:T(4,128)} all-gather(f32[5,8,4,128]{3,2,1,0:T(4,128)} %bitcast.26), channel_id=1, replica_groups=mesh['tile'=64,'mem'=8] {'mem'}, dimensions={1}, use_global_device_ids=true | all-gather | bytes 737280 | tf_op jit(solution)/shard_map/all_gather | solution.py:371
  21.3 12.3 %conditional.2 = (bf16[128,384]{1,0:T(8,128)(2,1)S(1)}) conditional(s32[]{:T(128)} %convert_element_type.4, () %tuple.18, (s32[64]{0:T(128)}, f32[128,128]{1,0:T(8,128)}) %tuple.19), branch_computations={%region_0.0_spmd, %region_1.0_spmd} | conditional | flops 300000000 | bytes 4393302 | solution.py:378
  21.3 1.3 dynamic_slice.4.scale_ref
  22.6 6.3 %reshape.22 = f32[64,2,64,2]{3,2,1,0:T(8,128)} reshape(f32[128,128]{1,0:T(8,128)} %get-tuple-element.20) | data formatting | bytes 131072 | tf_op jit(solution)/shard_map/cond/branch_1_fun/reshape | solution.py:375
  28.8 3.0 %copy.13 = f32[2,64,2,64]{3,2,1,0:T(2,128)S(1)} copy(f32[2,64,2,64]{2,3,0,1:T(8,128)} %bitcast.24) | data formatting | bytes 131072 | tf_op jit(solution)/shard_map/cond/branch_1_fun/transpose | solution.py:375
  31.8 0.1 reshape.23.smooth_y_ref
  32.0 1.6 prepare_y.1
  33.6 21.0 %adjoint.1.spent_ref = f32[64,64,128]{2,1,0:T(8,128)} custom-call(s32[1]{0:T(128)} %bitcast.2.core_ref, s32[64]{0:T(128)} %scale_ref.1, f32[5,64,4,128]{3,2,1,0:T(4,128)} %all_gather.3.dir_ref, bf16[5,64,64,128]{3,2,1,0:T(8,128)(2,1)} %bitcast.21, f32[64,64]{1,0:T(8,128)} %matrix_ref.3, f32[256,256]{1,0:T(8,128)S(1)} %copy-done.3, ...), custom_call_target="tpu_custom_call" | custom-call | flops 300000000 | bytes 4000000 | tf_op jit(solution)/shard_map/adjoint/pallas_call | solution.py:379
  54.6 0.0 copy-start.2
  54.6 0.0 copy-start.4
  54.6 13.8 %all-to-all-start = ((f32[64,64,128]{2,1,0:T(8,128)}), f32[64,64,128]{2,1,0:T(8,128)}, u32[]{:S(2)}, u32[]{:S(2)}) async-start(f32[64,64,128]{2,1,0:T(8,128)} %adjoint.1.spent_ref), calls=%async_computation | async-start | bytes 4194304 | tf_op jit(solution)/shard_map/all_to_all | solution.py:361
  68.5 0.1 conditional.3
  68.6 75.1 %all-to-all-done = f32[64,64,128]{2,1,0:T(8,128)} async-done(((f32[64,64,128]{2,1,0:T(8,128)}), f32[64,64,128]{2,1,0:T(8,128)}, u32[]{:S(2)}, u32[]{:S(2)}) %all-to-all-start) | async-done | bytes 2097184 | tf_op jit(solution)/shard_map/all_to_all | solution.py:361
  143.6 3.6 %smooth.1 = f32[64,64,128]{2,1,0:T(8,128)S(1)} custom-call(s32[1]{0:T(128)} %bitcast.2.core_ref, f32[4096,128]{1,0:T(8,128)} %bitcast.9.in_ref, bf16[128,384]{1,0:T(8,128)(2,1)S(1)} %get-tuple-element.29.y_ref, bf16[256,256]{1,0:T(8,128)(2,1)S(1)} %get-tuple-element.30.xh_ref, ...), custom_call_target="tpu_custom_call", output_to_operand_aliasing={{}: (5, {})} | custom-call | flops 1200000000 | bytes 4000000 | tf_op jit(solution)/shard_map/smooth/pallas_call | solution.py:386
  147.2 0.0 copy-start.1
  147.3 91.5 %all_to_all.15 = f32[64,64,128]{2,1,0:T(8,128)S(1)} all-to-all(f32[64,64,128]{2,1,0:T(8,128)S(1)} %smooth.1), channel_id=1, replica_groups=mesh['tile'=64,'mem'=8] {'tile'}, dimensions={0} | all-to-all | bytes 4194304 | tf_op jit(solution)/shard_map/all_to_all | solution.py:361
  238.7 0.0 copy-done.1
  238.7 1.9 give.1
  240.6 1.9 collective-permute-start
  242.6 1.9 keep.1
  244.4 0.0 collective-permute-done
  244.5 0.1 add.9
  244.6 9.9 %all_to_all.16.in_ref = f32[4,5,8,4,128]{4,3,2,1,0:T(4,128)S(1)} all-to-all(f32[4,5,8,4,128]{4,3,2,1,0:T(4,128)S(1)} %add.9), channel_id=1, replica_groups={{0,2,4,6},{1,3,5,7},{8,10,12,14},{9,11,13,15},{16,18,20,22},{17,19,21,2..., dimensions={0} | all-to-all | bytes 655360 | tf_op jit(solution)/shard_map/all_to_all | solution.py:390
  254.4 0.7 finish.1
  (8 shorter events, 0.0 us)
Async XLA Ops:
  21.3 12.3 %copy-start.3 = (f32[256,256]{1,0:T(8,128)S(1)}, f32[256,256]{1,0:T(8,128)}, u32[]{:S(2)}) copy-start(f32[256,256]{1,0:T(8,128)} %smooth_x_ref.1) | copy-start | bytes 786436
  54.6 13.9 %copy-start.2 = (f32[128,128]{1,0:T(8,128)S(1)}, f32[128,128]{1,0:T(8,128)}, u32[]{:S(2)}) copy-start(f32[128,128]{1,0:T(8,128)} %param.12) | copy-start | bytes 196612
  54.6 13.9 %copy-start.4 = (s32[64]{0:T(128)S(1)}, s32[64]{0:T(128)}, u32[]{:S(2)}) copy-start(s32[64]{0:T(128)} %scale_ref.1) | copy-start | bytes 772
  54.6 89.0 %all-to-all-start = ((f32[64,64,128]{2,1,0:T(8,128)}), f32[64,64,128]{2,1,0:T(8,128)}, u32[]{:S(2)}, u32[]{:S(2)}) async-start(f32[64,64,128]{2,1,0:T(8,128)} %adjoint.1.spent_ref), calls=%async_computation | async-start | bytes 4194304 | tf_op jit(solution)/shard_map/all_to_all | solution.py:361
  68.5 75.2 %copy-start = (f32[64,64,128]{2,1,0:T(8,128)S(1)}, f32[64,64,128]{2,1,0:T(8,128)}, u32[]{:S(2)}) copy-start(f32[64,64,128]{2,1,0:T(8,128)} %adjoint.1.spent_ref) | copy-start | bytes 6291460
  147.2 91.5 %copy-start.1 = (f32[64,64]{1,0:T(8,128)S(1)}, f32[64,64]{1,0:T(8,128)}, u32[]{:S(2)}) copy-start(f32[64,64]{1,0:T(8,128)} %matrix_ref.3) | copy-start | bytes 49156
  240.6 3.8 %collective-permute-start = (f32[4,5,8,4,128]{4,3,2,1,0:T(4,128)S(1)}, f32[4,5,8,4,128]{4,3,2,1,0:T(4,128)S(1)}, u32[]{:S(2)}, u32[]{:S(2)}) collective-permute-start(f32[4,5,8,4,128]{4,3,2,1,0:T(4,128)S(1)} %get-tuple-element.33), channel_id=1, source_target_pairs={{0,1},{1,0},{2,3},{3,2},{4,5},{5,4},{6,7},{7,6},{8,9},{9,8},{10,11... | collective-permute-start | bytes 983048 | tf_op jit(solution)/shard_map/ppermute | solution.py:389

commit v7 on v5

--- a/solution.py
+++ b/solution.py
@@ -173,9 +173,16 @@
     xl_ref[...] = low
 
 
-def smooth_kernel(core_ref, in_ref, y_ref, xh_ref, xl_ref, spent_ref, out_ref, source, result, out_sem):
+def smooth_kernel(core_ref, in_ref, y_ref, xh_ref, xl_ref, spent_ref, out_ref, source, result, in_sem, out_sem):
     del spent_ref
-    spread(in_ref, source)
+    view = source.reshape(LEVELS, PITCH, 128)
+    pieces = []
+    for c in range(4):
+        part = pl.ds(16 * c, 16)
+        pieces.append(pltpu.make_async_copy(in_ref.at[part], view.at[part, pl.ds(0, ROWS)], in_sem.at[c]))
+        pieces[c].start()
+    for piece in pieces:
+        piece.wait()
 
     def run(with_x):
         y_both, y_low = y_ref[:, :256], y_ref[:, 256:]
@@ -303,10 +310,10 @@
 smooth_call = call(
     smooth_kernel,
     "smooth",
-    [SMEM] + [VMEM] * 4 + [HBM],
+    [SMEM, HBM] + [VMEM] * 3 + [HBM],
     [(HBM, FIELDS)],
     1_200_000_000,
-    [SPREAD_SCRATCH, SPREAD_SCRATCH, DMA((4,))],
+    [SPREAD_SCRATCH, SPREAD_SCRATCH, DMA((4,)), DMA((4,))],
     vmem=48,
     aliases={5: 0},
 )
@@ -366,7 +373,7 @@
         lambda: list(prepare_call(*scale_and_y(), smooth_x)),
     )
 
-    smoothed = smooth_call(core, flat(exchange(adjoint)), cov_y, cov_xh, cov_xl, adjoint)
+    smoothed = smooth_call(core, exchange(adjoint), cov_y, cov_xh, cov_xl, adjoint)
     forward, give = give_call(core, flat(exchange(smoothed)), lines, vertical)
     keep = keep_call(core, forward, lines)
     both = keep + lax.ppermute(give, "mem", [(m, m ^ 1) for m in range(8)])

time: 258 us -> 257 us (level)
  no operation moved by 1% of the time
where the time goes in v7:
time: 257 us; the launch traced here: 255 us
  blocking collectives  123 us (48%)
  waiting for transfers between devices  77.1 us (30%)
  Pallas kernels  28.2 us (11%)
  starting transfers between devices  15.7 us (6%)
  local copies, waits for them, and re-layouts  10.7 us (4%)
    all_to_all x1, blocking collectives, exchange(): lax.all_to_all(fields, 'tile', split_axis=0, concat_axis=0, tiled=True)  91.6 us
    all_to_all x1, waiting for transfers between devices, exchange(): lax.all_to_all(fields, 'tile', split_axis=0, concat_axis=0, tiled=True)  77.1 us
    all_gather x1, blocking collectives, per_device(): full_dir = lax.all_gather(to_lines(search_dir), 'mem', axis=1, tiled=True)  21.3 us
    pallas_call x1, Pallas kernels, per_device(): adjoint_call(core, level_scale, full_dir, lines, vertical, smooth_x, early)  19 us
    all_to_all x1, starting transfers between devices, exchange(): lax.all_to_all(fields, 'tile', split_axis=0, concat_axis=0, tiled=True)  13.8 us
    all_to_all x1, blocking collectives, per_device(): lax.all_to_all(both, 'mem', split_axis=0, concat_axis=0, tiled=True, axis...  9.8 us
    reshape x2, local copies, waits for them, and re-layouts, scale_and_y(): smooth_y.reshape(64, 2, 64, 2).transpose(1, 0, 3, 2).reshape(128, 128)  6.38 us
  transfers between devices with their start and end apart: 2, of which 1 were waited for; matrix products, arithmetic and copies ran while one was open for 0% of the time, Pallas kernels for 1%

profile of v7, /device:TPU:1, one launch (start us, length us, event | category | flops | bytes accessed | tf_op | source)
XLA Modules:
  0.0 254.8 jit_solution(15516217026793458439)
XLA Ops:
  0.0 21.3 %all_gather.3.dir_ref = f32[5,64,4,128]{3,2,1,0:T(4,128)} all-gather(f32[5,8,4,128]{3,2,1,0:T(4,128)} %bitcast.25), channel_id=1, replica_groups=mesh['tile'=64,'mem'=8] {'mem'}, dimensions={1}, use_global_device_ids=true | all-gather | bytes 737280 | tf_op jit(solution)/shard_map/all_gather | solution.py:361
  21.3 12.3 %conditional.2 = (bf16[128,384]{1,0:T(8,128)(2,1)S(1)}) conditional(s32[]{:T(128)} %convert_element_type.4, () %tuple.18, (s32[64]{0:T(128)}, f32[128,128]{1,0:T(8,128)}) %tuple.19), branch_computations={%region_0.0_spmd, %region_1.0_spmd} | conditional | flops 300000000 | bytes 4393302 | solution.py:368
  21.3 1.3 dynamic_slice.4.scale_ref
  22.6 6.3 %reshape.20 = f32[64,2,64,2]{3,2,1,0:T(8,128)} reshape(f32[128,128]{1,0:T(8,128)} %get-tuple-element.20) | data formatting | bytes 131072 | tf_op jit(solution)/shard_map/cond/branch_1_fun/reshape | solution.py:365
  28.8 3.0 %copy.13 = f32[2,64,2,64]{3,2,1,0:T(2,128)S(1)} copy(f32[2,64,2,64]{2,3,0,1:T(8,128)} %bitcast.23) | data formatting | bytes 131072 | tf_op jit(solution)/shard_map/cond/branch_1_fun/transpose | solution.py:365
  31.8 0.1 reshape.21.smooth_y_ref
  32.0 1.6 prepare_y.1
  33.6 0.0 copy-done.3
  33.6 19.0 %adjoint.1.spent_ref = f32[64,64,128]{2,1,0:T(8,128)} custom-call(s32[1]{0:T(128)} %bitcast.2.core_ref, s32[64]{0:T(128)} %scale_ref.1, f32[5,64,4,128]{3,2,1,0:T(4,128)} %all_gather.3.dir_ref, bf16[5,64,64,128]{3,2,1,0:T(8,128)(2,1)} %bitcast.20, f32[64,64]{1,0:T(8,128)} %matrix_ref.3, f32[256,256]{1,0:T(8,128)S(1)} %copy-done.3, ...), custom_call_target="tpu_custom_call" | custom-call | flops 300000000 | bytes 4000000 | tf_op jit(solution)/shard_map/adjoint/pallas_call | solution.py:369
  52.5 0.0 copy-start.2
  52.6 0.0 copy-start.4
  52.6 13.8 %all-to-all-start = ((f32[64,64,128]{2,1,0:T(8,128)}), f32[64,64,128]{2,1,0:T(8,128)}, u32[]{:S(2)}, u32[]{:S(2)}) async-start(f32[64,64,128]{2,1,0:T(8,128)} %adjoint.1.spent_ref), calls=%async_computation | async-start | bytes 4194304 | tf_op jit(solution)/shard_map/all_to_all | solution.py:351
  66.4 0.1 conditional.3
  66.5 77.1 %all-to-all-done.in_ref = f32[64,64,128]{2,1,0:T(8,128)} async-done(((f32[64,64,128]{2,1,0:T(8,128)}), f32[64,64,128]{2,1,0:T(8,128)}, u32[]{:S(2)}, u32[]{:S(2)}) %all-to-all-start) | async-done | bytes 2097184 | tf_op jit(solution)/shard_map/all_to_all | solution.py:351
  143.6 3.2 %smooth.1 = f32[64,64,128]{2,1,0:T(8,128)S(1)} custom-call(s32[1]{0:T(128)} %bitcast.2.core_ref, f32[64,64,128]{2,1,0:T(8,128)} %all-to-all-done.in_ref, bf16[128,384]{1,0:T(8,128)(2,1)S(1)} %get-tuple-element.29.y_ref, bf16[256,256]{1,0:T(8,128)(2,1)S(1)} %get-tuple-element.30.xh_ref, ...), custom_call_target="tpu_custom_call", output_to_operand_aliasing={{}: (5, {})} | custom-call | flops 1200000000 | bytes 4000000 | tf_op jit(solution)/shard_map/smooth/pallas_call | solution.py:376
  146.9 0.0 copy-start.1
  146.9 91.6 %all_to_all.15 = f32[64,64,128]{2,1,0:T(8,128)S(1)} all-to-all(f32[64,64,128]{2,1,0:T(8,128)S(1)} %smooth.1), channel_id=1, replica_groups=mesh['tile'=64,'mem'=8] {'tile'}, dimensions={0} | all-to-all | bytes 4194304 | tf_op jit(solution)/shard_map/all_to_all | solution.py:351
  238.5 1.9 give.1
  240.4 1.9 collective-permute-start
  242.4 1.9 keep.1
  244.2 0.0 collective-permute-done
  244.3 0.1 add.9
  244.4 9.8 %all_to_all.16.in_ref = f32[4,5,8,4,128]{4,3,2,1,0:T(4,128)S(1)} all-to-all(f32[4,5,8,4,128]{4,3,2,1,0:T(4,128)S(1)} %add.9), channel_id=1, replica_groups={{0,2,4,6},{1,3,5,7},{8,10,12,14},{9,11,13,15},{16,18,20,22},{17,19,21,2..., dimensions={0} | all-to-all | bytes 655360 | tf_op jit(solution)/shard_map/all_to_all | solution.py:380
  254.2 0.7 finish.1
  (8 shorter events, 0.0 us)
Async XLA Ops:
  21.3 12.3 %copy-start.3 = (f32[256,256]{1,0:T(8,128)S(1)}, f32[256,256]{1,0:T(8,128)}, u32[]{:S(2)}) copy-start(f32[256,256]{1,0:T(8,128)} %smooth_x_ref.1) | copy-start | bytes 786436
  52.5 13.9 %copy-start.2 = (f32[128,128]{1,0:T(8,128)S(1)}, f32[128,128]{1,0:T(8,128)}, u32[]{:S(2)}) copy-start(f32[128,128]{1,0:T(8,128)} %param.12) | copy-start | bytes 196612
  52.6 13.9 %copy-start.4 = (s32[64]{0:T(128)S(1)}, s32[64]{0:T(128)}, u32[]{:S(2)}) copy-start(s32[64]{0:T(128)} %scale_ref.1) | copy-start | bytes 772
  52.6 91.1 %all-to-all-start = ((f32[64,64,128]{2,1,0:T(8,128)}), f32[64,64,128]{2,1,0:T(8,128)}, u32[]{:S(2)}, u32[]{:S(2)}) async-start(f32[64,64,128]{2,1,0:T(8,128)} %adjoint.1.spent_ref), calls=%async_computation | async-start | bytes 4194304 | tf_op jit(solution)/shard_map/all_to_all | solution.py:351
  66.4 77.2 %copy-start = (f32[64,64,128]{2,1,0:T(8,128)S(1)}, f32[64,64,128]{2,1,0:T(8,128)}, u32[]{:S(2)}) copy-start(f32[64,64,128]{2,1,0:T(8,128)} %adjoint.1.spent_ref) | copy-start | bytes 6291460
  146.9 91.7 %copy-start.1 = (f32[64,64]{1,0:T(8,128)S(1)}, f32[64,64]{1,0:T(8,128)}, u32[]{:S(2)}) copy-start(f32[64,64]{1,0:T(8,128)} %matrix_ref.3) | copy-start | bytes 49156
  240.4 3.8 %collective-permute-start = (f32[4,5,8,4,128]{4,3,2,1,0:T(4,128)S(1)}, f32[4,5,8,4,128]{4,3,2,1,0:T(4,128)S(1)}, u32[]{:S(2)}, u32[]{:S(2)}) collective-permute-start(f32[4,5,8,4,128]{4,3,2,1,0:T(4,128)S(1)} %get-tuple-element.33), channel_id=1, source_target_pairs={{0,1},{1,0},{2,3},{3,2},{4,5},{5,4},{6,7},{7,6},{8,9},{9,8},{10,11... | collective-permute-start | bytes 983048 | tf_op jit(solution)/shard_map/ppermute | solution.py:379
